TPU v7x, 32 devices: a whole 2x2x4 slice. The times are simulated.
32 devices in a mesh: tok: 4 (over z), row: 4 (over y, x), col: 2 (over core).
Axes of the slice: x: 2, y: 2, z: 4, core: 2. Of those that a mesh axis runs over, the one named last changes fastest.
Arguments:
- tokens: bfloat16 [16384, 768], P(('tok', 'row'), 'col'), may hold values from -6 to 6
- cotangent: bfloat16 [16384, 768], P(('tok', 'row'), 'col'), may hold values from -6 to 6
- lengths: int32 [4, 4], P('tok'), may hold values from 1 to 64, 128 in all within a row
- dealing: int32 [512], replicated, may hold values from 0 to 511, as said below
- project_in: bfloat16 [768, 3, 768], P('col', None, 'row'), may hold values from -0.21875 to 0.21875
- project_bias: bfloat16 [2, 768], P(None, 'row'), may hold values from -1.1953125 to 1.1953125
- project_out: bfloat16 [768, 768], P('row', 'col'), may hold values from -4 to 4
- output_bias: bfloat16 [768], P('col'), may hold values from -1.1953125 to 1.1953125
- first_gain: bfloat16 [768], P('col'), may hold values from 0.5 to 1.5
- first_shift: bfloat16 [768], P('col'), may hold values from -1.1953125 to 1.1953125
- up_weight: bfloat16 [768, 3072], P('col', 'row'), may hold values from -0.21875 to 0.21875
- up_bias: bfloat16 [3072], P('row'), may hold values from -1.1953125 to 1.1953125
- down_weight: bfloat16 [3072, 768], P('row', 'col'), may hold values from -0.109375 to 0.109375
- down_bias: bfloat16 [768], P('col'), may hold values from -1.1953125 to 1.1953125
- second_gain: bfloat16 [768], P('col'), may hold values from 0.5 to 1.5
- second_shift: bfloat16 [768], P('col'), may hold values from -1.1953125 to 1.1953125
Outputs:
- output: bfloat16 [16384, 768], P(('tok', 'row'), 'col')
- input_grad: bfloat16 [16384, 768], P(('tok', 'row'), 'col')
- project_in_grad: float32 [768, 3, 768], P('col', None, 'row')
- project_bias_grad: float32 [2, 768], P(None, 'row')
- project_out_grad: float32 [768, 768], P('row', 'col')
- output_bias_grad: float32 [768], P('col')
- first_gain_grad: float32 [768], P('col')
- first_shift_grad: float32 [768], P('col')
- up_weight_grad: float32 [768, 3072], P('col', 'row')
- up_bias_grad: float32 [3072], P('row')
- down_weight_grad: float32 [3072, 768], P('row', 'col')
- down_bias_grad: float32 [768], P('col')
- second_gain_grad: float32 [768], P('col')
- second_shift_grad: float32 [768], P('col')
Inputs may be any that keep to these rules, and one draw needn't show every extreme that they name: lengths[g] are the lengths, counted in blocks of 32 tokens, of group g's 4 sequences in the dealt order; every row sums to 128, and its largest is 64. dealing is a permutation of the blocks. Blocks are numbered in token order, and the blocks in [k * 32, (k + 1) * 32) form shard k, with row index k % 4 and group k // 4. A block keeps its row index: p and dealing[p] lie in shards of one row index. Each shard of the given order has exactly 8 of its blocks dealt into each group.
All inputs are finite; a program needn't handle non-finite values.
Results may differ from a plain program's by a relative error of at most 0.017.
Values may be sent and summed in bfloat16 or wider, within the bound.
No kernel may reach another device: no remote copies, remote signals or barrier semaphores. Data moves between devices by JAX's collectives and lax.ppermute only.
A program may use at most 192 MiB of HBM per device.

v0:
```python
from functools import partial
import math

import jax
import jax.numpy as jnp
from jax import lax
from jax.sharding import PartitionSpec as P

HEAD = 64


EPSILON = 1e-12
MASKED = -1000000000.0


def product(factor, operand):
    return jnp.dot(factor, operand, preferred_element_type=jnp.float32)


def product_tn(factor, operand):
    return lax.dot_general(
        factor, operand, (((0,), (0,)), ((), ())), preferred_element_type=jnp.float32
    )


def product_nt(factor, operand):
    return lax.dot_general(
        factor, operand, (((1,), (1,)), ((), ())), preferred_element_type=jnp.float32
    )


def rows_of(array, offset, amount):
    return lax.dynamic_slice_in_dim(array, offset, amount, 0)


def gather_rows(array):
    return lax.all_gather(array, "row", axis=0, tiled=True)


def gather_cols(array):
    return lax.all_gather(array, "col", axis=0, tiled=True)


def sum_rows(term, kept):
    return lax.psum_scatter(
        term(jnp.int32(0), kept * lax.axis_size("row")), "row", scatter_dimension=0, tiled=True
    )


def sum_cols(term, kept):
    return lax.psum_scatter(
        term(jnp.int32(0), kept * lax.axis_size("col")), "col", scatter_dimension=0, tiled=True
    )


def paired_sums(first, second):
    return lax.psum((first, second), "col")


def normalize(resid, gain, shift, width):
    totals, squares = paired_sums(jnp.sum(resid, axis=1), jnp.sum(resid * resid, axis=1))
    mean_value = totals / width
    variance = squares / width - mean_value * mean_value
    inverse = lax.rsqrt(variance + EPSILON)
    normed = (resid - mean_value[:, None]) * inverse[:, None]
    return (normed * gain + shift, normed, inverse)


def normalize_back(grad_normed, normed, inverse, width):
    first, second = paired_sums(jnp.sum(grad_normed, axis=1), jnp.sum(grad_normed * normed, axis=1))
    return inverse[:, None] * (
        grad_normed - first[:, None] / width - normed * (second[:, None] / width)
    )


def attend_forward(query_block, segment_block, key_all, value_all, segment, scale):
    matching = segment_block[:, None] == segment[None, :]
    outputs, maxima, totals = ([], [], [])
    for head_index in range(query_block.shape[1] // HEAD):
        columns = slice(head_index * HEAD, (head_index + 1) * HEAD)
        scores = jnp.where(
            matching, product_nt(query_block[:, columns], key_all[:, columns]) * scale, MASKED
        )
        maximum = jnp.max(scores, axis=1, keepdims=True)
        weights = jnp.exp(scores - maximum)
        total = jnp.sum(weights, axis=1, keepdims=True)
        shares = (weights / total).astype(jnp.bfloat16)
        outputs.append(product(shares, value_all[:, columns]))
        maxima.append(maximum)
        totals.append(total)
    return (
        jnp.concatenate(outputs, axis=1),
        jnp.concatenate(maxima, axis=1),
        jnp.concatenate(totals, axis=1),
    )


def attend_backward(carry, pieces, key_all, value_all, segment, scale):
    key_grad, value_grad = carry
    query_block, dout_block, maximum_block, total_block, segment_block = pieces
    matching = segment_block[:, None] == segment[None, :]
    query_parts, key_parts, value_parts = ([], [], [])
    for head_index in range(query_block.shape[1] // HEAD):
        columns = slice(head_index * HEAD, (head_index + 1) * HEAD)
        scores = jnp.where(
            matching, product_nt(query_block[:, columns], key_all[:, columns]) * scale, MASKED
        )
        weights = (
            jnp.exp(scores - maximum_block[:, head_index : head_index + 1])
            / total_block[:, head_index : head_index + 1]
        )
        shares = weights.astype(jnp.bfloat16)
        share_grads = product_nt(dout_block[:, columns], value_all[:, columns])
        centre = jnp.sum(weights * share_grads, axis=1, keepdims=True)
        score_grads = (weights * (share_grads - centre)).astype(jnp.bfloat16)
        query_parts.append(product(score_grads, key_all[:, columns]) * scale)
        key_parts.append(product_tn(score_grads, query_block[:, columns]) * scale)
        value_parts.append(product_tn(shares, dout_block[:, columns]))
    carry = (
        key_grad + jnp.concatenate(key_parts, axis=1),
        value_grad + jnp.concatenate(value_parts, axis=1),
    )
    return (carry, jnp.concatenate(query_parts, axis=1))


def local(
    tokens,
    cotangent,
    lengths,
    dealing,
    project_in,
    project_bias,
    project_out,
    output_bias,
    first_gain,
    first_shift,
    up_weight,
    up_bias,
    down_weight,
    down_bias,
    second_gain,
    second_shift,
):
    groups = lax.axis_size("tok")
    grid_rows = lax.axis_size("row")
    grid_cols = lax.axis_size("col")
    group_id = lax.axis_index("tok")
    row_id = lax.axis_index("row")
    col_id = lax.axis_index("col")
    shard_rows, half_width = tokens.shape
    width = half_width * grid_cols
    block_count = dealing.shape[0] // (groups * grid_rows)
    block_len = shard_rows // block_count
    per_pair = block_count // groups
    total_blocks = dealing.shape[0]
    inverse_deal = (
        jnp.zeros_like(dealing).at[dealing].set(jnp.arange(total_blocks, dtype=jnp.int32))
    )
    owners = (inverse_deal // (grid_rows * block_count)).reshape(groups, grid_rows, block_count)
    owner_row = lax.dynamic_index_in_dim(owners, row_id, 1, keepdims=False)
    my_targets = lax.dynamic_index_in_dim(owner_row, group_id, 0, keepdims=False)
    slot_ids = jnp.arange(block_count, dtype=jnp.int32)
    send_order = jnp.argsort(my_targets * block_count + slot_ids)
    shard_base = (group_id * grid_rows + row_id) * block_count
    sources = lax.dynamic_slice_in_dim(dealing, shard_base, block_count)
    source_group = sources // (grid_rows * block_count)
    source_slot = sources % block_count
    source_targets = jnp.take(owner_row, source_group, axis=0)
    earlier = (source_targets == group_id) & (slot_ids[None, :] < source_slot[:, None])
    arrival = source_group * per_pair + jnp.sum(earlier.astype(jnp.int32), axis=1)

    def reorder(array, order):
        blocks = array.reshape(block_count, block_len, array.shape[1])
        return jnp.take(blocks, order, axis=0).reshape(shard_rows, array.shape[1])

    sent_x, sent_dy = (
        lax.all_to_all(reorder(tokens, send_order), "tok", split_axis=0, concat_axis=0, tiled=True),
        lax.all_to_all(
            reorder(cotangent, send_order), "tok", split_axis=0, concat_axis=0, tiled=True
        ),
    )
    x_own = reorder(sent_x, arrival)
    dy_own = reorder(sent_dy, arrival)
    group_tokens = shard_rows * grid_rows
    half_rows = group_tokens // grid_cols
    ends = jnp.cumsum(lengths[0]) * block_len
    positions = jnp.arange(group_tokens, dtype=jnp.int32)
    segment = jnp.sum((positions[:, None] >= ends[None, :]).astype(jnp.int32), axis=1)
    query_segment = lax.dynamic_slice_in_dim(segment, col_id * half_rows, half_rows)
    head_width = project_bias.shape[1]
    scale = 1.0 / math.sqrt(HEAD)
    project_flat = project_in.reshape(half_width, 3 * head_width)
    x_full = gather_rows(x_own)
    joined = sum_cols(
        lambda offset, amount: product(rows_of(x_full, offset, amount), project_flat), half_rows
    )
    query = (joined[:, :head_width] + project_bias[0].astype(jnp.float32)).astype(jnp.bfloat16)
    key_half = joined[:, head_width : 2 * head_width].astype(jnp.bfloat16)
    value_half = (joined[:, 2 * head_width :] + project_bias[1].astype(jnp.float32)).astype(
        jnp.bfloat16
    )
    key_all, value_all = (
        lax.all_gather(key_half, "col", axis=0, tiled=True),
        lax.all_gather(value_half, "col", axis=0, tiled=True),
    )
    block_rows = min(512, half_rows)
    block_total = half_rows // block_rows
    query_blocks = query.reshape(block_total, block_rows, head_width)
    segment_blocks = query_segment.reshape(block_total, block_rows)
    mixed, maxima, totals = lax.map(
        lambda pieces: attend_forward(pieces[0], pieces[1], key_all, value_all, segment, scale),
        (query_blocks, segment_blocks),
    )
    heads_out = mixed.reshape(half_rows, head_width).astype(jnp.bfloat16)
    heads_all = gather_cols(heads_out)
    attention = sum_rows(
        lambda offset, amount: product(rows_of(heads_all, offset, amount), project_out), shard_rows
    )
    resid_one = x_own.astype(jnp.float32) + attention + output_bias.astype(jnp.float32)
    hidden, normed_one, inverse_one = normalize(
        resid_one, first_gain.astype(jnp.float32), first_shift.astype(jnp.float32), width
    )
    hidden_low = hidden.astype(jnp.bfloat16)
    hidden_full = gather_rows(hidden_low)
    upward = sum_cols(
        lambda offset, amount: product(rows_of(hidden_full, offset, amount), up_weight), half_rows
    ) + up_bias.astype(jnp.float32)
    activated, gelu_back = jax.vjp(partial(jax.nn.gelu, approximate=False), upward)
    act_low = activated.astype(jnp.bfloat16)
    act_full = gather_cols(act_low)
    downward = sum_rows(
        lambda offset, amount: product(rows_of(act_full, offset, amount), down_weight), shard_rows
    ) + down_bias.astype(jnp.float32)
    final, normed_two, inverse_two = normalize(
        hidden + downward, second_gain.astype(jnp.float32), second_shift.astype(jnp.float32), width
    )
    out_low = final.astype(jnp.bfloat16)
    grad_out = dy_own.astype(jnp.float32)
    second_gain_part = jnp.sum(grad_out * normed_two, axis=0)
    second_shift_part = jnp.sum(grad_out, axis=0)
    grad_two = normalize_back(
        grad_out * second_gain.astype(jnp.float32), normed_two, inverse_two, width
    )
    down_grad_low = grad_two.astype(jnp.bfloat16)
    down_grad_full = gather_rows(down_grad_low)
    down_weight_part = product_tn(act_full, down_grad_full)
    down_bias_part = jnp.sum(down_grad_full, axis=0, dtype=jnp.float32)
    act_grad = sum_cols(
        lambda offset, amount: product_nt(rows_of(down_grad_full, offset, amount), down_weight),
        half_rows,
    )
    up_grad_low = gelu_back(act_grad)[0].astype(jnp.bfloat16)
    up_grad_full = gather_cols(up_grad_low)
    up_weight_part = product_tn(hidden_full, up_grad_full)
    up_bias_part = jnp.sum(up_grad_full, axis=0, dtype=jnp.float32)
    grad_hidden = sum_rows(
        lambda offset, amount: product_nt(rows_of(up_grad_full, offset, amount), up_weight),
        shard_rows,
    )
    grad_hidden = grad_hidden + grad_two
    first_gain_part = jnp.sum(grad_hidden * normed_one, axis=0)
    first_shift_part = jnp.sum(grad_hidden, axis=0)
    grad_one = normalize_back(
        grad_hidden * first_gain.astype(jnp.float32), normed_one, inverse_one, width
    )
    attn_grad_low = grad_one.astype(jnp.bfloat16)
    attn_grad_full = gather_rows(attn_grad_low)
    project_out_part = product_tn(heads_all, attn_grad_full)
    output_bias_part = jnp.sum(attn_grad_full, axis=0, dtype=jnp.float32)
    mixed_grad = sum_cols(
        lambda offset, amount: product_nt(rows_of(attn_grad_full, offset, amount), project_out),
        half_rows,
    ).astype(jnp.bfloat16)
    zero_grads = (
        jnp.zeros((group_tokens, head_width), jnp.float32),
        jnp.zeros((group_tokens, head_width), jnp.float32),
    )
    (key_grad, value_grad), query_grad = lax.scan(
        lambda carry, pieces: attend_backward(carry, pieces, key_all, value_all, segment, scale),
        zero_grads,
        (
            query_blocks,
            mixed_grad.reshape(block_total, block_rows, head_width),
            maxima,
            totals,
            segment_blocks,
        ),
    )
    kv_grads = sum_cols(
        lambda offset, amount: jnp.concatenate(
            [rows_of(key_grad, offset, amount), rows_of(value_grad, offset, amount)], axis=1
        ),
        half_rows,
    )
    joined_grad = jnp.concatenate(
        [query_grad.reshape(half_rows, head_width), kv_grads], axis=1
    ).astype(jnp.bfloat16)
    joined_grad_full = gather_cols(joined_grad)
    project_in_part = product_tn(x_full, joined_grad_full).reshape(half_width, 3, head_width)
    project_bias_part = jnp.stack(
        [
            jnp.sum(joined_grad_full[:, :head_width], axis=0, dtype=jnp.float32),
            jnp.sum(joined_grad_full[:, 2 * head_width :], axis=0, dtype=jnp.float32),
        ]
    )
    input_part = sum_rows(
        lambda offset, amount: product_nt(rows_of(joined_grad_full, offset, amount), project_flat),
        shard_rows,
    )
    dealt_grad = (input_part + grad_one).astype(jnp.bfloat16)
    summed = (
        lax.psum(project_in_part.astype(jnp.bfloat16), "tok").astype(jnp.float32),
        lax.psum(project_bias_part.astype(jnp.bfloat16), "tok").astype(jnp.float32),
        lax.psum(project_out_part.astype(jnp.bfloat16), "tok").astype(jnp.float32),
        lax.psum(output_bias_part.astype(jnp.bfloat16), "tok").astype(jnp.float32),
        lax.psum(up_weight_part.astype(jnp.bfloat16), "tok").astype(jnp.float32),
        lax.psum(up_bias_part.astype(jnp.bfloat16), "tok").astype(jnp.float32),
        lax.psum(down_weight_part.astype(jnp.bfloat16), "tok").astype(jnp.float32),
        lax.psum(down_bias_part.astype(jnp.bfloat16), "tok").astype(jnp.float32),
    )
    norm_grads = lax.psum(
        (first_gain_part, first_shift_part, second_gain_part, second_shift_part), ("tok", "row")
    )
    back_order = jnp.argsort(arrival)
    returned_out, returned_grad = (
        lax.all_to_all(
            reorder(out_low, back_order), "tok", split_axis=0, concat_axis=0, tiled=True
        ),
        lax.all_to_all(
            reorder(dealt_grad, back_order), "tok", split_axis=0, concat_axis=0, tiled=True
        ),
    )
    restore = jnp.argsort(send_order)
    output = reorder(returned_out, restore)
    input_grad = reorder(returned_grad, restore)
    return (
        output,
        input_grad,
        summed[0],
        summed[1],
        summed[2],
        summed[3],
        norm_grads[0],
        norm_grads[1],
        summed[4],
        summed[5],
        summed[6],
        summed[7],
        norm_grads[2],
        norm_grads[3],
    )


def solution(mesh):
    in_specs = (
        P(("tok", "row"), "col"),
        P(("tok", "row"), "col"),
        P("tok", None),
        P(),
        P("col", None, "row"),
        P(None, "row"),
        P("row", "col"),
        P("col"),
        P("col"),
        P("col"),
        P("col", "row"),
        P("row"),
        P("row", "col"),
        P("col"),
        P("col"),
        P("col"),
    )
    out_specs = (
        P(("tok", "row"), "col"),
        P(("tok", "row"), "col"),
        P("col", None, "row"),
        P(None, "row"),
        P("row", "col"),
        P("col"),
        P("col"),
        P("col"),
        P("col", "row"),
        P("row"),
        P("row", "col"),
        P("col"),
        P("col"),
        P("col"),
    )
    return jax.shard_map(local, mesh=mesh, in_specs=in_specs, out_specs=out_specs, check_vma=False)
```

profile of v0, /device:TPU:0, one launch (start us, length us, event | category | flops | bytes accessed | tf_op | source)
XLA Modules:
  0.0 1422.8 jit_solution(654085981052166722)
XLA Ops:
  25.4 18.0 %all-to-all-done = bf16[4,256,384]{2,1,0:T(8,128)(2,1)S(1)} async-done(((bf16[4,256,384]{2,1,0:T(8,128)(2,1)}), bf16[4,256,384]{2,1,0:T(8,128)(2,1)S(1)}, u32[]{:S(2)}, u32[]{:S(2)}) %all-to-all-start) | async-done | bytes 786464 | tf_op jit(solution)/shard_map/all_to_all | solution.py:177
  45.2 43.2 %all-gather.11.cloned.1.call-done = bf16[4096,384]{1,0:T(8,128)(2,1)} async-done(((bf16[1024,384]{1,0:T(8,128)(2,1)}), bf16[4096,384]{1,0:T(8,128)(2,1)}) %all-gather.11.cloned.1.call-update) | async-done | bytes 3145744 | tf_op jit(solution)/shard_map/all_gather | solution.py:37
  95.4 17.9 %reduce-scatter.10.cloned.1.call-done = f32[2048,576]{0,1:T(8,128)} async-done(((f32[4096,576]{0,1:T(8,128)}), f32[2048,576]{0,1:T(8,128)}) %reduce-scatter.10.cloned.1.call-update) | async-done | bytes 4718608 | tf_op jit(solution)/shard_map/reduce_scatter | solution.py:51
  143.9 93.4 %while.29 = (s32[]{:T(128)}, bf16[4,512,192]{1,2,0:T(8,128)(2,1)S(1)}, f32[4,512,3]{1,2,0:T(4,128)S(1)}, f32[4,512,3]{1,2,0:T(4,128)S(1)}, s32[4,512]{1,0:T(4,12...) while((s32[]{:T(128)}, ...), condition=%wide.region_13.15_spmd, body=%wide.region_6.14_spmd.sunk | while | flops 1667828736 | bytes 83284088 | solution.py:210
  238.4 11.1 all-gather.17.cloned.1.call-done
  255.5 70.9 %reduce-scatter.12.cloned.1.call-done = f32[1024,384]{1,0:T(8,128)} async-done(((f32[4096,384]{1,0:T(8,128)}), f32[1024,384]{1,0:T(8,128)}) %reduce-scatter.12.cloned.1.call-update) | async-done | bytes 1572880 | tf_op jit(solution)/shard_map/reduce_scatter | solution.py:45
  332.1 44.1 %all-gather.19.cloned.1.call-done = bf16[4096,384]{1,0:T(8,128)(2,1)} async-done(((bf16[1024,384]{1,0:T(8,128)(2,1)}), bf16[4096,384]{1,0:T(8,128)(2,1)}) %all-gather.19.cloned.1.call-update) | async-done | bytes 3145744 | tf_op jit(solution)/shard_map/all_gather | solution.py:37
  386.7 21.0 %reduce-scatter.14.cloned.1.call-done = f32[2048,768]{1,0:T(8,128)} async-done(((f32[4096,768]{1,0:T(8,128)}), f32[2048,768]{1,0:T(8,128)}) %reduce-scatter.14.cloned.1.call-update) | async-done | bytes 6291472 | tf_op jit(solution)/shard_map/reduce_scatter | solution.py:51
  407.7 16.0 %multiply_convert_fusion.3 = (bf16[2048,768]{1,0:T(8,128)(2,1)}, f32[2048,768]{1,0:T(8,128)}) fusion(f32[2048,768]{1,0:T(8,128)} %reduce-scatter.14.cloned.1.call-done, f32[768]{0:T(1024)S(1)} %convert_element_type.174), kind=kLoop, calls=%fused_computation.109 | loop fusion | flops 103809024 | bytes 15731712 | tf_op jit(solution)/shard_map/convert_element_type | solution.py:229
  423.8 18.0 %all-gather.21.cloned.1.call-done = bf16[4096,768]{1,0:T(8,128)(2,1)} async-done(((bf16[2048,768]{1,0:T(8,128)(2,1)}), bf16[4096,768]{1,0:T(8,128)(2,1)}) %all-gather.21.cloned.1.call-update) | async-done | bytes 6291472 | tf_op jit(solution)/shard_map/all_gather | solution.py:41
  456.0 20.3 %all-to-all-done.2 = bf16[4,256,384]{2,1,0:T(8,128)(2,1)S(1)} async-done(((bf16[4,256,384]{2,1,0:T(8,128)(2,1)}), bf16[4,256,384]{2,1,0:T(8,128)(2,1)S(1)}, u32[]{:S(2)}, u32[]{:S(2)}) %all-to-all-start.2) | async-done | bytes 786464 | tf_op jit(solution)/shard_map/all_to_all | solution.py:178
  478.3 44.0 %reduce-scatter.16.cloned.1.call-done = f32[1024,384]{1,0:T(8,128)} async-done(((f32[4096,384]{1,0:T(8,128)}), f32[1024,384]{1,0:T(8,128)}) %reduce-scatter.16.cloned.1.call-update) | async-done | bytes 1572880 | tf_op jit(solution)/shard_map/reduce_scatter | solution.py:45
  535.9 44.1 %all-gather.23.cloned.1.call-done = bf16[4096,384]{1,0:T(8,128)(2,1)} async-done(((bf16[1024,384]{1,0:T(8,128)(2,1)}), bf16[4096,384]{1,0:T(8,128)(2,1)}) %all-gather.23.cloned.1.call-update) | async-done | bytes 3145744 | tf_op jit(solution)/shard_map/all_gather | solution.py:37
  590.0 21.6 %reduce-scatter.18.cloned.1.call-done = f32[2048,768]{1,0:T(8,128)} async-done(((f32[4096,768]{1,0:T(8,128)}), f32[2048,768]{1,0:T(8,128)}) %reduce-scatter.18.cloned.1.call-update) | async-done | bytes 6291472 | tf_op jit(solution)/shard_map/reduce_scatter | solution.py:51
  621.4 18.0 %all-gather.25.cloned.1.call-done = bf16[4096,768]{1,0:T(8,128)(2,1)} async-done(((bf16[2048,768]{1,0:T(8,128)(2,1)}), bf16[4096,768]{1,0:T(8,128)(2,1)}) %all-gather.25.cloned.1.call-update) | async-done | bytes 6291472 | tf_op jit(solution)/shard_map/all_gather | solution.py:41
  649.0 70.9 %reduce-scatter.20.cloned.1.call-done = f32[1024,384]{1,0:T(8,128)} async-done(((f32[4096,384]{1,0:T(8,128)}), f32[1024,384]{1,0:T(8,128)}) %reduce-scatter.20.cloned.1.call-update) | async-done | bytes 1572880 | tf_op jit(solution)/shard_map/reduce_scatter | solution.py:45
  729.9 44.1 %all-gather.27.cloned.1.call-done = bf16[4096,384]{1,0:T(8,128)(2,1)} async-done(((bf16[1024,384]{1,0:T(8,128)(2,1)}), bf16[4096,384]{1,0:T(8,128)(2,1)}) %all-gather.27.cloned.1.call-update) | async-done | bytes 3145744 | tf_op jit(solution)/shard_map/all_gather | solution.py:37
  778.8 11.0 reduce-scatter.22.cloned.1.call-done
  793.6 371.9 %while.30 = (s32[]{:T(128)}, f32[4096,192]{0,1:T(8,128)}, f32[4096,192]{0,1:T(8,128)}, bf16[4,512,192]{1,2,0:T(8,128)(2,1)}, s32[4,512]{1,0:T(4,128)S(1)}, /*ind...) while((s32[]{:T(128)}, f32[4096,192]{0,1:T(8,128)}, ...), condition=%wide.region_42.44_spmd.clone, body=%wide.region_38.43_spmd.clone.sunk | while | flops 4103600640 | bytes 390007232 | solution.py:278
  1172.9 14.6 %reduce-scatter.24.cloned.1.call-done = f32[2048,384]{0,1:T(8,128)} async-done(((f32[4096,384]{0,1:T(8,128)}), f32[2048,384]{0,1:T(8,128)}) %reduce-scatter.24.cloned.1.call-update) | async-done | bytes 3145744 | tf_op jit(solution)/shard_map/reduce_scatter | solution.py:51
  1191.6 15.7 %all-gather.29.cloned.1.call-done = bf16[4096,576]{0,1:T(8,128)(2,1)} async-done(((bf16[2048,576]{0,1:T(8,128)(2,1)}), bf16[4096,576]{0,1:T(8,128)(2,1)}) %all-gather.29.cloned.1.call-update) | async-done | bytes 4718608 | tf_op jit(solution)/shard_map/all_gather | solution.py:41
  1235.5 51.6 %reduce-scatter.26.cloned.1.call-done = f32[1024,384]{1,0:T(8,128)} async-done(((f32[4096,384]{1,0:T(8,128)}), f32[1024,384]{1,0:T(8,128)}) %reduce-scatter.26.cloned.1.call-update) | async-done | bytes 1572880 | tf_op jit(solution)/shard_map/reduce_scatter | solution.py:45
  1302.2 25.5 %all-to-all-done.1 = bf16[4,256,384]{2,1,0:T(8,128)(2,1)S(1)} async-done(((bf16[4,256,384]{2,1,0:T(8,128)(2,1)}), bf16[4,256,384]{2,1,0:T(8,128)(2,1)S(1)}, u32[]{:S(2)}, u32[]{:S(2)}) %all-to-all-start.1) | async-done | bytes 786464 | tf_op jit(solution)/shard_map/all_to_all | solution.py:326
  1339.3 47.7 %all-reduce = (f32[384]{0:T(512)}, f32[384]{0:T(512)}, f32[384]{0:T(512)}, f32[384]{0:T(512)}) all-reduce(f32[384]{0:T(512)S(1)} %copy-done.27, f32[384]{0:T(512)S(1)} %copy-done.28, f32[384]{0:T(512)S(1)} %copy-done.26, f32[384]{0:T(512)S(1)} %copy-done.25), channel_id=1, replica_groups=mesh['tok'=4,'row'=4,'col'=2] {'tok','row'}, use_global_device_ids=true, to_apply=%region_53.55 | all-reduce | flops 1536 | bytes 12288 | tf_op jit(solution)/shard_map/psum | solution.py:321
  (481 shorter events, 700.8 us)
Async XLA Ops:
  16.9 26.4 %all-to-all-start = ((bf16[4,256,384]{2,1,0:T(8,128)(2,1)}), bf16[4,256,384]{2,1,0:T(8,128)(2,1)S(1)}, u32[]{:S(2)}, u32[]{:S(2)}) async-start(bf16[4,256,384]{2,1,0:T(8,128)(2,1)} %bitcast.14), calls=%async_computation | async-start | bytes 1572864 | tf_op jit(solution)/shard_map/all_to_all | solution.py:177
  23.3 65.1 %all-gather.11.cloned.1.call-start = ((), (), s32[]{:S(2)}) async-start(), calls=%async_computation.13 | async-start | bytes 3932160 | tf_op jit(solution)/shard_map/all_gather | solution.py:37
  45.2 68.2 %reduce-scatter.10.cloned.1.call-start = ((), (), s32[]{:S(2)}) async-start(), calls=%async_computation.14 | async-start | bytes 14155776 | tf_op jit(solution)/shard_map/reduce_scatter | solution.py:51
  95.4 31.6 %all-gather.13.cloned.1.call-start = ((), (), s32[]{:S(2)}) async-start(), calls=%async_computation.15 | async-start | bytes 2359296 | tf_op jit(solution)/shard_map/all_gather | solution.py:203
  115.7 24.2 %all-gather.15.cloned.1.call-start = ((), (), s32[]{:S(2)}) async-start(), calls=%async_computation.16 | async-start | bytes 2359296 | tf_op jit(solution)/shard_map/all_gather | solution.py:204
  118.8 130.7 %all-gather.17.cloned.1.call-start = ((), (), s32[]{:S(2)}) async-start(), calls=%async_computation.17 | async-start | bytes 2359296 | tf_op jit(solution)/shard_map/all_gather | solution.py:41
  238.3 88.1 %reduce-scatter.12.cloned.1.call-start = ((), (), s32[]{:S(2)}) async-start(), calls=%async_computation.18 | async-start | bytes 7864320 | tf_op jit(solution)/shard_map/reduce_scatter | solution.py:45
  254.9 121.3 %all-gather.19.cloned.1.call-start = ((), (), s32[]{:S(2)}) async-start(), calls=%async_computation.19 | async-start | bytes 3932160 | tf_op jit(solution)/shard_map/all_gather | solution.py:37
  332.0 75.7 %reduce-scatter.14.cloned.1.call-start = ((), (), s32[]{:S(2)}) async-start(), calls=%async_computation.20 | async-start | bytes 18874368 | tf_op jit(solution)/shard_map/reduce_scatter | solution.py:51
  386.0 55.8 %all-gather.21.cloned.1.call-start = ((), (), s32[]{:S(2)}) async-start(), calls=%async_computation.21 | async-start | bytes 9437184 | tf_op jit(solution)/shard_map/all_gather | solution.py:41
  423.8 98.5 %reduce-scatter.16.cloned.1.call-start = ((), (), s32[]{:S(2)}) async-start(), calls=%async_computation.22 | async-start | bytes 7864320 | tf_op jit(solution)/shard_map/reduce_scatter | solution.py:45
  450.7 25.6 %all-to-all-start.2 = ((bf16[4,256,384]{2,1,0:T(8,128)(2,1)}), bf16[4,256,384]{2,1,0:T(8,128)(2,1)S(1)}, u32[]{:S(2)}, u32[]{:S(2)}) async-start(bf16[4,256,384]{2,1,0:T(8,128)(2,1)} %bitcast.27), calls=%async_computation.6 | async-start | bytes 1572864 | tf_op jit(solution)/shard_map/all_to_all | solution.py:178
  455.7 124.2 %all-gather.23.cloned.1.call-start = ((), (), s32[]{:S(2)}) async-start(), calls=%async_computation.23 | async-start | bytes 3932160 | tf_op jit(solution)/shard_map/all_gather | solution.py:37
  535.8 75.7 %reduce-scatter.18.cloned.1.call-start = ((), (), s32[]{:S(2)}) async-start(), calls=%async_computation.24 | async-start | bytes 18874368 | tf_op jit(solution)/shard_map/reduce_scatter | solution.py:51
  589.9 49.4 %all-gather.25.cloned.1.call-start = ((), (), s32[]{:S(2)}) async-start(), calls=%async_computation.25 | async-start | bytes 9437184 | tf_op jit(solution)/shard_map/all_gather | solution.py:41
  621.3 98.5 %reduce-scatter.20.cloned.1.call-start = ((), (), s32[]{:S(2)}) async-start(), calls=%async_computation.26 | async-start | bytes 7864320 | tf_op jit(solution)/shard_map/reduce_scatter | solution.py:45
  648.3 125.7 %all-gather.27.cloned.1.call-start = ((), (), s32[]{:S(2)}) async-start(), calls=%async_computation.27 | async-start | bytes 3932160 | tf_op jit(solution)/shard_map/all_gather | solution.py:37
  729.8 60.0 %reduce-scatter.22.cloned.1.call-start = ((), (), s32[]{:S(2)}) async-start(), calls=%async_computation.28 | async-start | bytes 4718592 | tf_op jit(solution)/shard_map/reduce_scatter | solution.py:51
  778.8 408.8 %reduce-scatter.24.cloned.1.call-start = ((), (), s32[]{:S(2)}) async-start(), calls=%async_computation.29 | async-start | bytes 9437184 | tf_op jit(solution)/shard_map/reduce_scatter | solution.py:51
  1171.7 35.5 %all-gather.29.cloned.1.call-start = ((), (), s32[]{:S(2)}) async-start(), calls=%async_computation.30 | async-start | bytes 7077888 | tf_op jit(solution)/shard_map/all_gather | solution.py:41
  1191.5 95.6 %reduce-scatter.26.cloned.1.call-start = ((), (), s32[]{:S(2)}) async-start(), calls=%async_computation.31 | async-start | bytes 7864320 | tf_op jit(solution)/shard_map/reduce_scatter | solution.py:45
  1290.8 37.0 %all-to-all-start.1 = ((bf16[4,256,384]{2,1,0:T(8,128)(2,1)}), bf16[4,256,384]{2,1,0:T(8,128)(2,1)S(1)}, u32[]{:S(2)}, u32[]{:S(2)}) async-start(bf16[4,256,384]{2,1,0:T(8,128)(2,1)} %bitcast.23), calls=%async_computation.5 | async-start | bytes 1572864 | tf_op jit(solution)/shard_map/all_to_all | solution.py:326
  1295.3 109.5 %all-reduce.9.cloned.1.call-start = ((), (), s32[]{:S(2)}) async-start(), calls=%async_computation.32 | async-start | bytes 3538944 | tf_op jit(solution)/shard_map/psum | solution.py:312
  1327.8 85.8 %all-to-all-start.3 = ((bf16[4,256,384]{2,1,0:T(8,128)(2,1)}), bf16[4,256,384]{2,1,0:T(8,128)(2,1)S(1)}, u32[]{:S(2)}, u32[]{:S(2)}) async-start(bf16[4,256,384]{2,1,0:T(8,128)(2,1)} %bitcast.32), calls=%async_computation.12 | async-start | bytes 1572864 | tf_op jit(solution)/shard_map/all_to_all | solution.py:329
  (75 other events, 1112.4 us)
Sparse Core Ops, SparseCore 0:
  45.3 43.0 all-gather.10
  95.5 17.7 reduce-scatter.9
  115.9 11.0 all-gather.12
  129.0 10.9 all-gather.14
  238.4 10.9 all-gather.16
  255.0 71.3 reduce-scatter.11
  332.1 43.9 all-gather.18
  386.2 21.4 reduce-scatter.13
  423.9 17.8 all-gather.20
  450.9 71.3 reduce-scatter.15
  536.0 43.9 all-gather.22
  590.0 21.4 reduce-scatter.17
  621.4 17.8 all-gather.24
  648.4 71.3 reduce-scatter.19
  730.0 43.9 all-gather.26
  778.9 10.8 reduce-scatter.21
  1171.9 15.6 reduce-scatter.23
  1191.6 15.5 all-gather.28
  1215.6 71.4 reduce-scatter.25
  1302.4 97.5 all-reduce.8
where the time goes:
time: 1430 us; the launch traced here: 1420 us
  waiting for transfers between devices  641 us (45%)
  matrix products  385 us (27%)
  other arithmetic  216 us (15%)
  blocking collectives  68.2 us (5%)
  local copies, waits for them, and re-layouts  58.2 us (4%)
  starting transfers between devices  20.5 us (1%)
  loops' own time  17.7 us (1%)
  between operations  15.1 us (1%)
    reduce_scatter x4, waiting for transfers between devices, sum_rows(): lax.psum_scatter(term(jnp.int32(0), kept * lax.axis_size('row')), 'row',...  237 us
    dot_general x40, matrix products, product_nt(): lax.dot_general(factor, operand, (((1,), (1,)), ((), ())), preferred_elem...  185 us
    all_gather x4, waiting for transfers between devices, gather_rows(): return lax.all_gather(array, 'row', axis=0, tiled=True)  175 us
    dot_general x28, matrix products, product(): return jnp.dot(factor, operand, preferred_element_type=jnp.float32)  103 us
    dot_general x28, matrix products, product_tn(): lax.dot_general(factor, operand, (((0,), (0,)), ((), ())), preferred_elem...  96.7 us
    convert_element_type x12, other arithmetic, attend_backward(): score_grads = (weights * (share_grads - centre)).astype(jnp.bfloat16)  95.1 us
    reduce_scatter x5, waiting for transfers between devices, sum_cols(): lax.psum_scatter(term(jnp.int32(0), kept * lax.axis_size('col')), 'col',...  86.1 us
    all_gather x4, waiting for transfers between devices, gather_cols(): return lax.all_gather(array, 'col', axis=0, tiled=True)  62.8 us
  transfers between devices with their start and end apart: 24, of which 22 were waited for; matrix products, arithmetic and copies ran while one was open for 4% of the time, Pallas kernels for 0%

commit v1 on v0

v1 whole, which is shorter than its diff:
```python
from functools import partial

import jax
import jax.numpy as jnp
from jax import lax
from jax.experimental import pallas as pl
from jax.experimental.pallas import tpu as pltpu
from jax.sharding import PartitionSpec as P

HEAD = 64
LANES = 128
EPSILON = 1e-12
OFF = -1000000000.0
BF = jnp.bfloat16
F32 = jnp.float32
VMEM_LIMIT = 60 * 1024 * 1024


def nn(a, b):
    return lax.dot_general(a, b, (((1,), (0,)), ((), ())), preferred_element_type=F32)


def nt(a, b):
    return lax.dot_general(a, b, (((1,), (1,)), ((), ())), preferred_element_type=F32)


def tn(a, b):
    return lax.dot_general(a, b, (((0,), (0,)), ((), ())), preferred_element_type=F32)


def call(kernel, outs, spaces, scratch=(), flops=0, moved=0):
    memory = {"s": pltpu.SMEM, "v": pltpu.VMEM}
    return pl.pallas_call(
        kernel,
        out_shape=[jax.ShapeDtypeStruct(shape, dtype) for shape, dtype in outs],
        in_specs=[pl.BlockSpec(memory_space=memory[s]) for s in spaces],
        out_specs=[pl.BlockSpec(memory_space=pltpu.VMEM) for _ in outs],
        scratch_shapes=list(scratch),
        compiler_params=pltpu.CompilerParams(vmem_limit_bytes=VMEM_LIMIT),
        cost_estimate=pl.CostEstimate(flops=flops, bytes_accessed=moved, transcendentals=0),
    )


def rows_at(block, size):
    return pl.ds(pl.multiple_of(block * size, size), size)


def send_kernel(sizes, deal, where, x, *outs):
    groups, grid_rows, count, block = sizes
    g, r = where[0], where[1]
    mine = g * grid_rows + r
    for d in range(groups):
        base = (lax.rem(g + d, groups) * grid_rows + r) * count

        def step(j, rank):
            source = deal[base + j]
            hit = lax.div(source, count) == mine

            @pl.when(hit)
            def _():
                outs[d][rows_at(rank, block), :] = x[rows_at(lax.rem(source, count), block), :]

            return rank + hit.astype(jnp.int32)

        lax.fori_loop(0, count, step, jnp.int32(0))


def final_kernel(sizes, deal, where, *refs):
    groups, grid_rows, count, block = sizes
    pieces, out = refs[:groups], refs[groups]
    g, r = where[0], where[1]
    mine = g * grid_rows + r
    for d in range(groups):
        base = (lax.rem(g + groups - d, groups) * grid_rows + r) * count

        def step(j, rank):
            source = deal[base + j]
            hit = lax.div(source, count) == mine

            @pl.when(hit)
            def _():
                out[rows_at(lax.rem(source, count), block), :] = pieces[d][rows_at(rank, block), :]

            return rank + hit.astype(jnp.int32)

        lax.fori_loop(0, count, step, jnp.int32(0))


def home_of(j, run, c):
    turn = lax.div(j, run)
    return lax.rem(turn, 2), lax.div(turn, 2) * run + lax.rem(j, run)


def arrive_kernel(sizes, run, deal, where, *refs):
    groups, grid_rows, count, block = sizes
    pieces, own, other, ranks = refs[:groups], refs[groups], refs[groups + 1], refs[groups + 2]
    g, r, c = where[0], where[1], where[2]
    base = (g * grid_rows + r) * count
    for d in range(groups):
        origin = lax.rem(g + groups - d, groups)

        def step(j, rank):
            hit = lax.div(deal[base + j], grid_rows * count) == origin

            @pl.when(hit)
            def _():
                core, place = home_of(j, run, c)
                rows = pieces[d][rows_at(rank, block), :]

                @pl.when(core == c)
                def _():
                    own[rows_at(place, block), :] = rows

                @pl.when(core != c)
                def _():
                    other[rows_at(place, block), :] = rows

            return rank + hit.astype(jnp.int32)

        lax.fori_loop(0, count, step, jnp.int32(0))


def return_kernel(sizes, run, deal, where, own, other, *outs):
    groups, grid_rows, count, block = sizes
    g, r, c = where[0], where[1], where[2]
    base = (g * grid_rows + r) * count
    for d in range(groups):
        origin = lax.rem(g + d, groups)

        def step(j, rank):
            hit = lax.div(deal[base + j], grid_rows * count) == origin

            @pl.when(hit)
            def _():
                core, place = home_of(j, run, c)

                @pl.when(core == c)
                def _():
                    outs[d][rows_at(rank, block), :] = own[rows_at(place, block), :]

                @pl.when(core != c)
                def _():
                    outs[d][rows_at(rank, block), :] = other[rows_at(place, block), :]

            return rank + hit.astype(jnp.int32)

        lax.fori_loop(0, count, step, jnp.int32(0))


def sequence_ends(lengths, number):
    ends, total = [], jnp.int32(0)
    for s in range(number):
        total = total + lengths[0, s]
        ends.append(total)
    return ends


def sequence_of(ends, block):
    return sum((block >= end).astype(jnp.int32) for end in ends)


def first_of(ends, block):
    start = jnp.int32(0)
    for end in ends:
        start = jnp.where(block >= end, end, start)
    return start


def last_of(ends, block):
    stop = ends[-1]
    for end in reversed(ends):
        stop = jnp.where(block < end, end, stop)
    return stop


def thirds(v):
    one = v.astype(BF)
    rest = v - one.astype(F32)
    two = rest.astype(BF)
    three = (rest - two.astype(F32)).astype(BF)
    return one.astype(F32), two.astype(F32), three.astype(F32)


def attend_kernel(sizes, chunk_blocks, heads, seqs, run, deal, where, lengths, *refs):
    groups, grid_rows, count, block = sizes
    chunks = len(chunk_blocks)
    pieces = refs[: chunks * grid_rows * 2]
    weights = refs[chunks * grid_rows * 2 : chunks * grid_rows * 2 + 2]
    bias = refs[chunks * grid_rows * 2 + 2]
    outs = refs[chunks * grid_rows * 2 + 3 :]
    q_ref, k_ref, v_ref, o_ref, xq_ref, own_ref = outs[:6]
    mixed = outs[6 : 6 + grid_rows]
    place, tally = outs[6 + grid_rows :]
    g, r, c = where[0], where[1], where[2]
    ends = sequence_ends(lengths, seqs)
    per_pair = count // groups
    for k in range(grid_rows):
        row = r ^ k
        for d in range(groups):
            tally[d] = 0

        def step(j, carry):
            origin = lax.div(deal[(g * grid_rows + row) * count + j], grid_rows * count)
            d = lax.rem(g - origin + groups, groups)
            rank = tally[d]
            tally[d] = rank + 1
            place[k, d * per_pair + rank] = row * count + j
            return carry

        lax.fori_loop(0, count, step, jnp.int32(0))
    lane = lax.broadcasted_iota(jnp.int32, (block, HEAD), 1)
    ones_v = jnp.where(lane < 3, 1.0, 0.0)
    tail_k = (lane >= seqs) & (lane < seqs + 3)
    w0, w1 = weights[0][...], weights[1][...]
    q_bias, v_bias = bias[0:1, :].astype(F32), bias[1:2, :].astype(F32)
    unit = 8
    start = 0
    for chunk, blocks in enumerate(chunk_blocks):
        for k in range(grid_rows):
            x0, x1 = pieces[(chunk * grid_rows + k) * 2], pieces[(chunk * grid_rows + k) * 2 + 1]
            for part in range(blocks // unit):
                span = slice(part * unit * block, (part + 1) * unit * block)
                joined = nt(x0[span, :], w0) + nt(x1[span, :], w1)
                for b in range(unit):
                    at = place[k, start + part * unit + b]
                    seg = sequence_of(ends, at)
                    core, local = home_of(at, run, c)
                    inside = slice(b * block, (b + 1) * block)
                    key_tail = jnp.where((lane == seg) | tail_k, 1.0, 0.0)
                    for h in range(heads):
                        left = h * 3 * HEAD
                        key = joined[inside, left + HEAD : left + 2 * HEAD]
                        value = joined[inside, left + 2 * HEAD : left + 3 * HEAD] + v_bias[:, h * HEAD : (h + 1) * HEAD]
                        k_ref[h, rows_at(at, block), :] = jnp.concatenate([key, key_tail], axis=1).astype(BF)
                        v_ref[h, rows_at(at, block), :] = jnp.concatenate([value, ones_v], axis=1).astype(BF)

                    @pl.when(core == c)
                    def _():
                        query_tail = jnp.where((lane < seqs) & (lane != seg), OFF, 0.0)
                        for h in range(heads):
                            left = h * 3 * HEAD
                            query = joined[inside, left : left + HEAD] + q_bias[:, h * HEAD : (h + 1) * HEAD]
                            query = query.astype(BF).astype(F32) * (HEAD**-0.5)
                            q_ref[h, rows_at(local, block), :] = jnp.concatenate([query, query_tail], axis=1).astype(BF)
                        here = slice((part * unit + b) * block, (part * unit + b + 1) * block)
                        xq_ref[rows_at(local, block), : x0.shape[1]] = x0[here, :]
                        xq_ref[rows_at(local, block), x0.shape[1] :] = x1[here, :]

        start += blocks
    rows = run * block
    local_runs = q_ref.shape[1] // rows
    shard_runs = local_runs // grid_rows
    own_ref[...] = xq_ref[rows_at(r, rows * shard_runs), :]
    wide = 2
    lane_q = lax.broadcasted_iota(jnp.int32, (rows, LANES), 1)
    for h in range(heads):

        def one_run(i, carry):
            first = i * 2 * run + c * run
            low = lax.div(first_of(ends, first), wide * run)
            high = lax.div(last_of(ends, first + run - 1) + wide * run - 1, wide * run)
            query = q_ref[h, rows_at(i, rows), :]

            def keys(j, state):
                top, acc = state
                scores = nt(query, k_ref[h, rows_at(j, wide * rows), :])
                peak = jnp.maximum(top, jnp.max(scores, axis=1, keepdims=True))
                part = jnp.exp(scores - peak).astype(BF)
                acc = acc * jnp.exp(top - peak) + nn(part, v_ref[h, rows_at(j, wide * rows), :])
                return peak, acc

            top, acc = lax.fori_loop(
                low, high, keys, (jnp.full((rows, 1), -3e38, F32), jnp.zeros((rows, LANES), F32))
            )
            total = acc[:, HEAD : HEAD + 1]
            o_ref[h, rows_at(i, rows), :] = (acc[:, :HEAD] / total).astype(BF)
            terms = thirds(top + jnp.log(total))
            kept = query.astype(F32)
            for t, term in enumerate(terms):
                kept = jnp.where(lane_q == HEAD + seqs + t, -term, kept)
            q_ref[h, rows_at(i, rows), :] = kept.astype(BF)
            return carry

        lax.fori_loop(0, local_runs, one_run, jnp.int32(0))
    for k in range(grid_rows):
        cells = [
            o_ref[h, rows_at((r ^ k) * shard_runs + half, rows), :] for half in range(shard_runs) for h in range(heads)
        ]
        mixed[k][...] = jnp.concatenate(cells, axis=1)


def attend_back_kernel(grid_rows, heads, seqs, run, block, where, lengths, q_ref, k_ref, v_ref, o_ref, *refs):
    grads = refs[:grid_rows]
    dq_ref, own_ref, other_ref, do_ref, acc_ref, key_acc, value_acc = refs[grid_rows:]
    r, c = where[1], where[2]
    ends = sequence_ends(lengths, seqs)
    rows = run * block
    local_runs = q_ref.shape[1] // rows
    shard_runs = local_runs // grid_rows
    lane = lax.broadcasted_iota(jnp.int32, (rows, HEAD), 1)
    for k in range(grid_rows):
        for half in range(shard_runs):
            at = rows_at((r ^ k) * shard_runs + half, rows)
            for h in range(heads):
                left = (half * heads + h) * HEAD
                grad = grads[k][:, left : left + HEAD].astype(F32)
                centre = jnp.sum(grad * o_ref[h, at, :].astype(F32), axis=1, keepdims=True)
                tail = jnp.zeros((rows, HEAD), F32)
                for t, term in enumerate(thirds(centre)):
                    tail = jnp.where(lane == t, -term, tail)
                do_ref[h, at, :] = jnp.concatenate([grad, tail], axis=1).astype(BF)
    for h in range(heads):
        acc_ref[...] = jnp.zeros_like(acc_ref)

        def key_run(i, core):
            low = first_of(ends, i * run)
            high = last_of(ends, i * run + run - 1)
            key = k_ref[h, rows_at(i, rows), :]
            value = v_ref[h, rows_at(i, rows), :]
            key_acc[...] = jnp.zeros_like(key_acc)
            value_acc[...] = jnp.zeros_like(value_acc)

            def query_run(j, carry):
                query = q_ref[h, rows_at(j, rows), :]
                grad = do_ref[h, rows_at(j, rows), :]
                shares = jnp.exp(nt(key, query))
                score_grads = (shares * nt(value, grad)).astype(BF)
                value_acc[...] += nn(shares.astype(BF), grad)
                key_acc[...] += nn(score_grads, query)
                acc_ref[rows_at(j, rows), :] += tn(score_grads, key)
                return carry

            lax.fori_loop(
                lax.div(low - c * run + run, 2 * run), lax.div(high - c * run + 2 * run - 1, 2 * run), query_run, jnp.int32(0)
            )
            return jnp.concatenate([key_acc[:, :HEAD], value_acc[:, :HEAD]], axis=1)

        def pair(i, carry):
            own_ref[h, rows_at(i, rows), :] = key_run(2 * i + c, 0)
            other_ref[h, rows_at(i, rows), :] = key_run(2 * i + 1 - c, 1).astype(BF)
            return carry

        lax.fori_loop(0, local_runs, pair, jnp.int32(0))
        dq_ref[h, :, :] = (acc_ref[:, :HEAD] * (HEAD**-0.5)).astype(BF)


def join_kernel(grid_rows, heads, where, dq_ref, own_ref, got_ref, *refs):
    pieces, joined = refs[:grid_rows], refs[grid_rows]
    r = where[1]
    rows = pieces[0].shape[0] // heads
    shard_runs = pieces[0].shape[1] // (3 * HEAD)
    for k in range(grid_rows):
        for h in range(heads):
            cells = []
            for half in range(shard_runs):
                at = rows_at((r ^ k) * shard_runs + half, rows)
                both = (own_ref[h, at, :] + got_ref[h, at, :].astype(F32)).astype(BF)
                cells += [dq_ref[h, at, :], both]
                joined[at, h * 3 * HEAD : (h + 1) * 3 * HEAD] = jnp.concatenate([dq_ref[h, at, :], both], axis=1)
            pieces[k][h * rows : (h + 1) * rows, :] = jnp.concatenate(cells, axis=1)


def project_in_grad_kernel(joined, xq, own, other):
    half = own.shape[1]
    wide = joined.shape[1]
    total = jnp.sum(joined[...].astype(F32), axis=0, keepdims=True)
    pad = jnp.zeros((1, 2 * half - wide), F32)
    total = jnp.concatenate([total, pad], axis=1)
    below = own.shape[0] - wide
    sums = jnp.concatenate([total[:, :half], total[:, half:], jnp.zeros((below - 2, half), F32)], axis=0).astype(BF)
    own[:wide, :] = tn(joined[...], xq[:, :half]).astype(BF)
    other[:wide, :] = tn(joined[...], xq[:, half:]).astype(BF)
    own[wide:, :] = sums
    other[wide:, :] = sums


def middle_kernel(plan, grid_rows, where, *refs):
    at = 0

    def take(n):
        nonlocal at
        got = refs[at : at + n]
        at += n
        return got

    mixed = take(grid_rows)
    (x_ref,) = take(1)
    dy = take(2)
    first = take(2 * grid_rows)
    second = take(2 * grid_rows)
    outs = take(2)
    act_ref, up_grad_ref, hidden_ref, down_grad_ref, attn_grad_ref, grad_one_ref = take(6)
    mixed_grad = take(grid_rows)
    (small,) = take(1)
    (slope_ref,) = take(1)
    half = dy[0].shape[1]
    width = 2 * half
    inner = mixed[0].shape[1] // 2
    rows = mixed[0].shape[0]
    r, c = where[1], where[2]
    small[...] = jnp.zeros_like(small)

    def vector(index):
        row = plan["vectors"] + index
        return jnp.concatenate([second[0][row : row + 1, :], second[1][row : row + 1, :]], axis=1).astype(F32)

    output_bias, first_gain, first_shift, down_bias, second_gain, second_shift = (vector(i) for i in range(6))

    def mean(v):
        return jnp.sum(v, axis=1, keepdims=True) / width

    def norm(v):
        centred = v - mean(v)
        inverse = lax.rsqrt(mean(centred * centred) + EPSILON)
        return centred * inverse, inverse

    def norm_back(v, normed, inverse):
        return inverse * (v - mean(v) - normed * mean(v * normed))

    def total(v):
        return jnp.sum(v, axis=0, keepdims=True)

    def keep(row, v):
        small[row : row + 1, :] += v

    for part in range(2):
        span = slice(part * rows, (part + 1) * rows)
        lanes = slice(part * inner, (part + 1) * inner)
        parts = []
        for j in range(2):
            parts.append(sum(nn(mixed[k][:, lanes], first[2 * k + j][plan["out"], :]) for k in range(grid_rows)))
        attention = jnp.concatenate(parts, axis=1) + output_bias
        normed_one, inverse_one = norm(x_ref[span, :].astype(F32) + attention)
        hidden = normed_one * first_gain + first_shift
        low = hidden.astype(BF)
        hidden_ref[span, :] = low
        downs = [jnp.zeros((rows, half), F32), jnp.zeros((rows, half), F32)]
        for k in range(grid_rows):
            for u in range(2):
                cols = slice((2 * k + u) * half, (2 * k + u + 1) * half)
                up_rows = plan["up"][u]
                upward = nn(low[:, :half], first[2 * k][up_rows, :]) + nn(low[:, half:], first[2 * k + 1][up_rows, :])
                upward = upward + first[2 * k][plan["up_bias"] + u : plan["up_bias"] + u + 1, :].astype(F32)
                bell = (1.0 + lax.erf(upward * (2.0**-0.5))) * 0.5
                slope_ref[:, cols] = bell + upward * jnp.exp(upward * upward * -0.5) * 0.3989422804014327
                act = (upward * bell).astype(BF)
                act_ref[span, cols] = act
                down_rows = plan["down"][u]
                for j in range(2):
                    downs[j] = downs[j] + nn(act, second[2 * k + j][down_rows, :])
        downward = jnp.concatenate(downs, axis=1) + down_bias
        normed_two, inverse_two = norm(hidden + downward)
        final = (normed_two * second_gain + second_shift).astype(BF)
        outs[0][span, :] = final[:, :half]
        outs[1][span, :] = final[:, half:]
        grad_out = jnp.concatenate([dy[0][span, :], dy[1][span, :]], axis=1).astype(F32)
        keep(0, total(grad_out * normed_two))
        keep(1, total(grad_out))
        grad_two = norm_back(grad_out * second_gain, normed_two, inverse_two)
        down_grad = grad_two.astype(BF)
        down_grad_ref[span, :] = down_grad
        keep(4, total(down_grad.astype(F32)))
        grads = [grad_two[:, :half], grad_two[:, half:]]
        for k in range(grid_rows):
            for u in range(2):
                cols = slice((2 * k + u) * half, (2 * k + u + 1) * half)
                up_rows, down_rows = plan["up"][u], plan["down"][u]
                act_grad = nt(down_grad[:, :half], second[2 * k][down_rows, :]) + nt(
                    down_grad[:, half:], second[2 * k + 1][down_rows, :]
                )
                up_grad = (act_grad * slope_ref[:, cols]).astype(BF)
                up_grad_ref[span, cols] = up_grad
                row = pl.ds(8 + (r ^ k), 1)
                small[row, u * half : (u + 1) * half] += total(up_grad.astype(F32))
                for j in range(2):
                    grads[j] = grads[j] + nt(up_grad, first[2 * k + j][up_rows, :])
        grad_hidden = jnp.concatenate(grads, axis=1)
        keep(2, total(grad_hidden * normed_one))
        keep(3, total(grad_hidden))
        grad_one = norm_back(grad_hidden * first_gain, normed_one, inverse_one)
        grad_one_ref[span, :] = grad_one
        attn_grad = grad_one.astype(BF)
        attn_grad_ref[span, :] = attn_grad
        keep(5, total(attn_grad.astype(F32)))
        for k in range(grid_rows):
            back = nt(attn_grad[:, :half], first[2 * k][plan["out"], :]) + nt(
                attn_grad[:, half:], first[2 * k + 1][plan["out"], :]
            )
            mixed_grad[k][:, lanes] = back.astype(BF)
    sums = small[:8, :]
    small[:8, :] = jnp.where(c == 0, sums, jnp.concatenate([sums[:, half:], sums[:, :half]], axis=1))


def middle_grad_kernel(plan, grid_rows, *refs):
    mixed = refs[:grid_rows]
    act, up_grad, hidden, down_grad, attn_grad = refs[grid_rows : grid_rows + 5]
    first, second = refs[grid_rows + 5 : grid_rows + 7], refs[grid_rows + 7 : grid_rows + 9]
    half = hidden.shape[1] // 2
    rows, inner = mixed[0].shape[0], mixed[0].shape[1] // 2
    for j in range(2):
        side = slice(j * half, (j + 1) * half)
        for place, k in enumerate(plan["second_order"]):
            for u in range(2):
                cols = slice((2 * k + u) * half, (2 * k + u + 1) * half)
                second[j][place, plan["down"][u], :] = tn(act[:, cols], down_grad[:, side]).astype(BF)
        for place, k in enumerate(plan["first_order"]):
            for u in range(2):
                cols = slice((2 * k + u) * half, (2 * k + u + 1) * half)
                first[j][place, plan["up"][u], :] = tn(hidden[:, side], up_grad[:, cols]).astype(BF)
            back = tn(mixed[k][:, :inner], attn_grad[:rows, side]) + tn(mixed[k][:, inner:], attn_grad[rows:, side])
            first[j][place, plan["out"], :] = back.astype(BF)


def input_grad_kernel(plan, grid_rows, heads, *refs):
    pieces = refs[:grid_rows]
    second = refs[grid_rows : 3 * grid_rows]
    grad_one, own, other = refs[3 * grid_rows :]
    half = own.shape[1]
    rows = pieces[0].shape[0] // heads
    wide = 3 * HEAD
    for part in range(2):
        span = slice(part * rows, (part + 1) * rows)
        for j, out in enumerate((own, other)):
            total = grad_one[span, j * half : (j + 1) * half]
            for k in range(grid_rows):
                for h in range(heads):
                    top = plan["join"] + h * wide
                    total = total + nn(
                        pieces[k][h * rows : (h + 1) * rows, part * wide : (part + 1) * wide],
                        second[2 * k + j][top : top + wide, :],
                    )
            out[span, :] = total.astype(BF)


def shift(array, axis, to):
    return lax.ppermute(array, axis, [(i, to(i)) for i in range(lax.axis_size(axis))])


def to_row(array, k):
    return shift(array, "row", lambda i: i ^ k)


def to_col(array):
    return shift(array, "col", lambda i: 1 - i)


def after(array, *earlier):
    return lax.optimization_barrier((array, *earlier))[0]


def gather_row(array, turn):
    near, side = to_row(array, 1), to_row(array, 2)
    far = to_row(near, 2) if turn == 0 else to_row(side, 1)
    return [array, near, side, far]


def add(*arrays):
    return sum(a.astype(F32) for a in arrays).astype(BF)


def reduce_row(own, got, turn):
    first, then = (1, 2) if turn == 0 else (2, 1)
    came = to_row(add(own[2:], got[2:]), first)
    last = to_row(add(own[1], got[1], came[1]), then)
    return add(own[0], got[0], came[0], last)


def reduce_groups(array, group):
    if lax.axis_size("tok") != 4:
        return lax.psum(array, "tok")
    side = (group ^ (group >> 1)) & 1
    middle = array.shape[0] // 2
    low, high = array[:middle], array[middle:]
    half = add(jnp.where(side == 0, low, high), shift(jnp.where(side == 0, high, low), "tok", lambda i: i ^ 1))
    half = add(half, shift(half, "tok", lambda i: i ^ 3))
    rest = shift(half, "tok", lambda i: i ^ 1)
    return jnp.concatenate([jnp.where(side == 0, half, rest), jnp.where(side == 0, rest, half)], axis=0)


def local(
    tokens,
    cotangent,
    lengths,
    dealing,
    project_in,
    project_bias,
    project_out,
    output_bias,
    first_gain,
    first_shift,
    up_weight,
    up_bias,
    down_weight,
    down_bias,
    second_gain,
    second_shift,
):
    groups, grid_rows = lax.axis_size("tok"), lax.axis_size("row")
    group, row, col = lax.axis_index("tok"), lax.axis_index("row"), lax.axis_index("col")
    where = jnp.stack([group, row, col]).astype(jnp.int32)
    shard_rows, half = tokens.shape
    width = 2 * half
    count = dealing.shape[0] // (groups * grid_rows)
    block = shard_rows // count
    sizes = (groups, grid_rows, count, block)
    seqs = lengths.shape[1]
    inner = project_bias.shape[1]
    heads = inner // HEAD
    hidden_part = up_weight.shape[1]
    run = count // 4
    rows = run * block
    own_rows = shard_rows // 2
    half_rows = own_rows * grid_rows
    wide = 3 * inner
    piece = (shard_rows // groups, half)
    shard = (shard_rows, half)

    def exchange(pieces):
        return [shift(p, "tok", lambda i, d=d: (i + d) % groups) if d else p for d, p in enumerate(pieces)]

    def send(array):
        return exchange(call(partial(send_kernel, sizes), [(piece, BF)] * groups, "ssv")(dealing, where, array))

    def send_back(own, other):
        pieces = call(partial(return_kernel, sizes, run), [(piece, BF)] * groups, "ssvv")(dealing, where, own, other)
        got = exchange(pieces)
        return call(partial(final_kernel, sizes), [(shard, BF)], "ss" + "v" * groups)(dealing, where, *got)[0]

    joined_weight = (
        project_in.transpose(1, 2, 0).reshape(3, heads, HEAD, half).transpose(1, 0, 2, 3).reshape(wide, half)
    )
    vectors = jnp.stack([output_bias, first_gain, first_shift, down_bias, second_gain, second_shift])
    up_bias_rows = up_bias.reshape(2, half)
    first_weights = jnp.concatenate(
        [up_weight[:, :half], up_weight[:, half:], project_out, jnp.pad(up_bias_rows, ((0, 14), (0, 0)))], axis=0
    )
    second_weights = jnp.concatenate([down_weight, joined_weight, jnp.pad(vectors, ((0, 10), (0, 0)))], axis=0)
    plan = {
        "up": (slice(0, half), slice(half, 2 * half)),
        "out": slice(2 * half, 2 * half + inner),
        "up_bias": 2 * half + inner,
        "down": (slice(0, half), slice(half, 2 * half)),
        "join": hidden_part,
        "vectors": hidden_part + wide,
        "first_order": (0, 2, 1, 3),
        "second_order": (0, 1, 2, 3),
    }

    got = send(tokens)
    if groups == 4:
        chunks, chunk_blocks = got, [count // groups] * groups
    else:
        chunks, chunk_blocks = [jnp.concatenate(got, axis=0)], [count]
    pieces = []
    for turn, chunk in enumerate(chunks):
        for part in gather_row(chunk, turn % 2):
            pieces += [part, to_col(part)]
    q, k, v, mixed_own, xq, x_own, *mixed = call(
        partial(attend_kernel, sizes, chunk_blocks, heads, seqs, run),
        [
            ((heads, half_rows, LANES), BF),
            ((heads, 2 * half_rows, LANES), BF),
            ((heads, 2 * half_rows, LANES), BF),
            ((heads, half_rows, HEAD), BF),
            ((half_rows, width), BF),
            ((own_rows, width), BF),
        ]
        + [((rows, 2 * inner), BF)] * grid_rows,
        "sss" + "v" * (len(pieces) + 3),
        [pltpu.SMEM((grid_rows, count), jnp.int32), pltpu.SMEM((groups,), jnp.int32)],
    )(dealing, where, lengths, *pieces, joined_weight, to_col(joined_weight), project_bias)

    dy_got = send(after(cotangent, *got))
    dy_own, dy_other = call(
        partial(arrive_kernel, sizes, run), [((own_rows, half), BF)] * 2, "ss" + "v" * groups,
        [pltpu.SMEM((groups,), jnp.int32)],
    )(dealing, where, *dy_got)
    dy = [dy_own, to_col(dy_other)]

    firsts, seconds = [], []
    for part in gather_row(first_weights, 0):
        firsts += [part, to_col(part)]
    for part in gather_row(second_weights, 1):
        seconds += [part, to_col(part)]

    mixed_got = [to_row(m, i) if i else m for i, m in enumerate(mixed)]
    hidden_all = grid_rows * hidden_part
    out0, out1, act, up_grad, hidden, down_grad, attn_grad, grad_one, *rest = call(
        partial(middle_kernel, plan, grid_rows),
        [
            ((own_rows, half), BF),
            ((own_rows, half), BF),
            ((own_rows, hidden_all), BF),
            ((own_rows, hidden_all), BF),
            ((own_rows, width), BF),
            ((own_rows, width), BF),
            ((own_rows, width), BF),
            ((own_rows, width), F32),
        ]
        + [((rows, 2 * inner), BF)] * grid_rows
        + [((8 + 8, width), F32)],
        "s" + "v" * (grid_rows + 3 + 4 * grid_rows),
        [pltpu.VMEM((rows, hidden_all), F32)],
    )(where, *mixed_got, x_own, *dy, *firsts, *seconds)
    mixed_grad, small = rest[:grid_rows], rest[grid_rows]
    mixed_grad_got = [to_row(m, i) if i else m for i, m in enumerate(mixed_grad)]
    small = lax.psum(small, ("tok", "row", "col"))

    first_rows = 2 * half + inner
    first_own, first_other, second_own, second_other = call(
        partial(middle_grad_kernel, plan, grid_rows),
        [((grid_rows, first_rows, half), BF)] * 2 + [((grid_rows, hidden_part, half), BF)] * 2,
        "v" * (grid_rows + 5),
    )(*mixed_got, act, up_grad, hidden, down_grad, attn_grad)
    first_sum = reduce_groups(reduce_row(first_own, to_col(first_other), 0), group)
    second_sum = reduce_groups(reduce_row(second_own, to_col(second_other), 1), group)

    output = send_back(out0, to_col(out1))

    dq, kv_own, kv_other = call(
        partial(attend_back_kernel, grid_rows, heads, seqs, run, block),
        [
            ((heads, half_rows, HEAD), BF),
            ((heads, half_rows, LANES), F32),
            ((heads, half_rows, LANES), BF),
        ],
        "ss" + "v" * (4 + grid_rows),
        [
            pltpu.VMEM((heads, half_rows, LANES), BF),
            pltpu.VMEM((half_rows, LANES), F32),
            pltpu.VMEM((rows, LANES), F32),
            pltpu.VMEM((rows, LANES), F32),
        ],
    )(where, lengths, q, k, v, mixed_own, *mixed_grad_got)
    *joined_pieces, joined = call(
        partial(join_kernel, grid_rows, heads),
        [((heads * rows, 2 * 3 * HEAD), BF)] * grid_rows + [((half_rows, wide), BF)],
        "svvv",
    )(where, dq, kv_own, to_col(kv_other))
    joined_got = [to_row(m, i) if i else m for i, m in enumerate(joined_pieces)]
    in_own, in_other = call(project_in_grad_kernel, [((wide + 32, half), BF)] * 2, "vv")(joined, xq)
    in_sum = reduce_groups(add(in_own, to_col(in_other)), group)
    dx_own, dx_other = call(
        partial(input_grad_kernel, plan, grid_rows, heads),
        [((own_rows, half), BF)] * 2,
        "v" * (3 * grid_rows + 1),
    )(*joined_got, *seconds, grad_one)
    input_grad = send_back(dx_own, to_col(dx_other))

    project_in_grad = (
        in_sum[:wide].reshape(heads, 3, HEAD, half).transpose(1, 0, 2, 3).reshape(3, inner, half).transpose(2, 0, 1)
    )
    sums = in_sum[wide : wide + 2].reshape(2 * half)[:wide].reshape(heads, 3, HEAD)
    project_bias_grad = jnp.stack([sums[:, 0].reshape(inner), sums[:, 2].reshape(inner)])
    up_bias_grad = lax.dynamic_slice_in_dim(small, 8 + row, 1, 0)[0]
    vector_grads = lax.dynamic_slice_in_dim(small[:8], col * half, half, 1)
    return (
        output,
        input_grad,
        project_in_grad.astype(F32),
        project_bias_grad.astype(F32),
        first_sum[2 * half :].astype(F32),
        vector_grads[5],
        vector_grads[2],
        vector_grads[3],
        jnp.concatenate([first_sum[:half], first_sum[half : 2 * half]], axis=1).astype(F32),
        up_bias_grad,
        second_sum.astype(F32),
        vector_grads[4],
        vector_grads[0],
        vector_grads[1],
    )


def solution(mesh):
    stream, grid = P(("tok", "row"), "col"), P("row", "col")
    joined, mids, cols = P("col", None, "row"), P("col", "row"), P("col")
    in_specs = (
        stream, stream, P("tok", None), P(), joined, P(None, "row"), grid, cols,
        cols, cols, mids, P("row"), grid, cols, cols, cols,
    )
    out_specs = (
        stream, stream, joined, P(None, "row"), grid, cols,
        cols, cols, mids, P("row"), grid, cols, cols, cols,
    )
    return jax.shard_map(local, mesh=mesh, in_specs=in_specs, out_specs=out_specs, check_vma=False)
```

time: 1430 us -> 622 us (0.43)
  waiting for transfers between devices: 641 us -> 140 us
  matrix products: 385 us -> 0 us
  Pallas kernels: 0 us -> 295 us
  other arithmetic: 216 us -> 20.7 us
  starting transfers between devices: 20.5 us -> 105 us
  local copies, waits for them, and re-layouts: 58.2 us -> 10.8 us
  loops' own time: 17.7 us -> 0 us
  blocking collectives: 68.2 us -> 51.5 us
    dot_general x96 -> x0, matrix products: 385 us -> none  [the longest x40 185 us: product_nt(): lax.dot_general(factor, operand, (((1,), (1,)), ((), ())), preferred_elem...]
    reduce_scatter x9 -> x0, waiting for transfers between devices: 323 us -> none  [the longest x4 237 us: sum_rows(): lax.psum_scatter(term(jnp.int32(0), kept * lax.axis_size('row')), 'row',...]
    pallas_call x0 -> x14, Pallas kernels: none -> 295 us  [the longest x1 106 us: local(): call(partial(attend_back_kernel, grid_rows, heads, seqs, run, block), [((...]
    all_gather x10 -> x0, waiting for transfers between devices: 254 us -> none  [the longest x4 175 us: gather_rows(): return lax.all_gather(array, 'row', axis=0, tiled=True)]
    ppermute x0 -> x84, waiting for transfers between devices: none -> 140 us  [shift(): lax.ppermute(array, axis, [(i, to(i)) for i in range(lax.axis_size(axis))])]
    convert_element_type x35 -> x18, other arithmetic: 144 us -> 17.8 us  [the longest x13 14.2 us: add(): return sum((a.astype(F32) for a in arrays)).astype(BF)]
    ppermute x0 -> x84, starting transfers between devices: none -> 105 us  [shift(): lax.ppermute(array, axis, [(i, to(i)) for i in range(lax.axis_size(axis))])]
    all_to_all x4 -> x0, waiting for transfers between devices: 63.9 us -> none  [the longest x1 25.5 us: local(): lax.all_to_all(reorder(out_low, back_order), 'tok', split_axis=0, concat_...]
  transfers between devices with their start and end apart: 24 -> 84, of which waited for: 22 -> 27; matrix products, arithmetic and copies ran while one was open for 4% -> 4% of each run, Pallas kernels for 0% -> 39%
where the time goes in v1:
time: 622 us; the launch traced here: 625 us
  Pallas kernels  295 us (47%)
  waiting for transfers between devices  140 us (23%)
  starting transfers between devices  105 us (17%)
  blocking collectives  51.5 us (8%)
  other arithmetic  20.7 us (3%)
  local copies, waits for them, and re-layouts  10.8 us (2%)
    ppermute x84, waiting for transfers between devices, shift(): lax.ppermute(array, axis, [(i, to(i)) for i in range(lax.axis_size(axis))])  140 us
    pallas_call x1, Pallas kernels, local(): call(partial(attend_back_kernel, grid_rows, heads, seqs, run, block), [((...  106 us
    ppermute x84, starting transfers between devices, shift(): lax.ppermute(array, axis, [(i, to(i)) for i in range(lax.axis_size(axis))])  105 us
    pallas_call x1, Pallas kernels, local(): call(partial(attend_kernel, sizes, chunk_blocks, heads, seqs, run), [((he...  86.7 us
    psum x1, blocking collectives, local(): small = lax.psum(small, ('tok', 'row', 'col'))  51.5 us
    pallas_call x1, Pallas kernels, local(): call(partial(middle_kernel, plan, grid_rows), [((own_rows, half), BF), ((...  33.7 us
    convert_element_type x13, other arithmetic, add(): return sum((a.astype(F32) for a in arrays)).astype(BF)  14.2 us
    pallas_call x1, Pallas kernels, local(): call(partial(middle_grad_kernel, plan, grid_rows), [((grid_rows, first_ro...  13.9 us
  transfers between devices with their start and end apart: 84, of which 27 were waited for; matrix products, arithmetic and copies ran while one was open for 4% of the time, Pallas kernels for 39%

profile of v1, /device:TPU:0, one launch (start us, length us, event | category | flops | bytes accessed | tf_op | source)
XLA Modules:
  0.0 625.2 jit_solution(6396716124716322352)
XLA Ops:
  20.7 7.0 %collective-permute-done.15.refs_16_ = bf16[256,384]{1,0:T(8,128)(2,1)S(1)} collective-permute-done((bf16[256,384]{1,0:T(8,128)(2,1)}, bf16[256,384]{1,0:T(8,128)(2,1)S(1)}, u32[]{:S(2)}, u32[]{:S(2)}) %collective-permute-start.15) | collective-permute-done | bytes 196640 | tf_op jit(solution)/shard_map/ppermute | solution.py:536
  52.2 6.0 collective-permute-done.27.refs_28_
  58.8 4.8 collective-permute-done.36.refs_2_
  70.4 24.5 %collective-permute-done.21.refs_22_ = bf16[256,384]{1,0:T(8,128)(2,1)S(1)} collective-permute-done((bf16[256,384]{1,0:T(8,128)(2,1)}, bf16[256,384]{1,0:T(8,128)(2,1)S(1)}, u32[]{:S(2)}, u32[]{:S(2)}) %collective-permute-start.21) | collective-permute-done | bytes 196640 | tf_op jit(solution)/shard_map/ppermute | solution.py:536
  97.0 6.7 %collective-permute-done.29.refs_30_ = bf16[256,384]{1,0:T(8,128)(2,1)} collective-permute-done((bf16[256,384]{1,0:T(8,128)(2,1)}, bf16[256,384]{1,0:T(8,128)(2,1)}, u32[]{:S(2)}, u32[]{:S(2)}) %collective-permute-start.29) | collective-permute-done | bytes 196640 | tf_op jit(solution)/shard_map/ppermute | solution.py:536
  104.4 4.8 shard_map.266
  112.1 86.7 %shard_map.264 = (bf16[3,2048,128]{2,1,0:T(8,128)(2,1)}, bf16[3,4096,128]{2,1,0:T(8,128)(2,1)}, bf16[3,4096,128]{2,1,0:T(8,128)(2,1)}, bf16[3,2048,64]{2,1,0:T(8...) custom-call(s32[512]{0:T(512)} %deal.15, ...), custom_call_target="tpu_custom_call" | custom-call | tf_op jit(solution)/shard_map/pallas_call | solution.py:658
  200.0 4.8 collective-permute-done.32.refs_1_
  205.3 8.6 %collective-permute-start.41 = (bf16[976,384]{1,0:T(8,128)(2,1)}, bf16[976,384]{1,0:T(8,128)(2,1)S(1)}, u32[]{:S(2)}, u32[]{:S(2)}) collective-permute-start(bf16[976,384]{1,0:T(8,128)(2,1)} %collective-permute-done.40.refs_9_), channel_id=1, source_target_pairs={{0,1},{1,0},{2,3},{3,2},{4,5},{5,4},{6,7},{7,6},{8,9},{9,8},{10,11... | collective-permute-start | bytes 2248712 | tf_op jit(solution)/shard_map/ppermute | solution.py:536
  220.7 12.0 %collective-permute-done.44.refs_13_ = bf16[976,384]{1,0:T(8,128)(2,1)S(1)} collective-permute-done((bf16[976,384]{1,0:T(8,128)(2,1)}, bf16[976,384]{1,0:T(8,128)(2,1)S(1)}, u32[]{:S(2)}, u32[]{:S(2)}) %collective-permute-start.44) | collective-permute-done | bytes 749600 | tf_op jit(solution)/shard_map/ppermute | solution.py:536
  238.1 33.7 %shard_map.267 = (bf16[512,384]{1,0:T(8,128)(2,1)}, bf16[512,384]{1,0:T(8,128)(2,1)}, bf16[512,3072]{1,0:T(8,128)(2,1)}, bf16[512,3072]{1,0:T(8,128)(2,1)}, bf16...) custom-call(s32[3]{0:T(128)} %pad_add_fusion.where, ...), custom_call_target="tpu_custom_call" | custom-call | tf_op jit(solution)/shard_map/pallas_call | solution.py:688
  271.8 13.9 %shard_map.276 = (bf16[4,960,384]{2,1,0:T(8,128)(2,1)}, bf16[4,960,384]{2,1,0:T(8,128)(2,1)}, bf16[4,768,384]{2,1,0:T(8,128)(2,1)}, bf16[4,768,384]{2,1,0:T(8,128)(2,1)}) custom-call(bf16[256,384]{1,0:T(8,128)(2,1)} %get-tuple-element.76.refs_0_, bf16[256,384]{1,0:T(8,128)(2,1)} %copy-done.9, bf16[256,384]{1,0:T(8,128)(2,1)} %copy-done.10, ...), custom_call_target="tpu_custom_call" | custom-call | tf_op jit(solution)/shard_map/pallas_call | solution.py:710
  298.3 106.3 %shard_map.270 = (bf16[3,2048,64]{2,1,0:T(8,128)(2,1)}, f32[3,2048,128]{2,1,0:T(8,128)}, bf16[3,2048,128]{2,1,0:T(8,128)(2,1)}) custom-call(s32[3]{0:T(128)} %pad_add_fusion.where, s32[1,4]{1,0:T(1,128)} %lengths.3, bf16[3,2048,128]{2,1,0:T(8,128)(2,1)} %get-tuple-element.94.q_ref, bf16[3,4096,128]{2,1,0:T(8,128)(2,1)} %get-tuple-element.95.k_ref, ...), custom_call_target="tpu_custom_call" | custom-call | tf_op jit(solution)/shard_map/pallas_call | solution.py:720
  404.6 20.1 %collective-permute-start.60 = (bf16[3,2048,128]{2,1,0:T(8,128)(2,1)}, bf16[3,2048,128]{2,1,0:T(8,128)(2,1)S(1)}, u32[]{:S(2)}, u32[]{:S(2)}) collective-permute-start(bf16[3,2048,128]{2,1,0:T(8,128)(2,1)} %get-tuple-element.104), channel_id=1, source_target_pairs={{0,1},{1,0},{2,3},{3,2},{4,5},{5,4},{6,7},{7,6},{8,9},{9,8},{10,11... | collective-permute-start | bytes 4718600 | tf_op jit(solution)/shard_map/ppermute | solution.py:536
  430.8 6.5 %shard_map.271 = (bf16[768,384]{1,0:T(8,128)(2,1)}, bf16[768,384]{1,0:T(8,128)(2,1)}, bf16[768,384]{1,0:T(8,128)(2,1)}, bf16[768,384]{1,0:T(8,128)(2,1)}, bf16[2048,576]{1,0:T(8,128)(2,1)}) custom-call(s32[3]{0:T(128)} %pad_add_fusion.where, bf16[3,2048,64]{2,1,0:T(8,128)(2,1)} %get-tuple-element.102.dq_ref, f32[3,2048,128]{2,1,0:T(8,128)} %get-tuple-element.103.own_ref, ...), custom_call_target="tpu_custom_call" | custom-call | tf_op jit(solution)/shard_map/pallas_call | solution.py:735
  437.3 6.3 %shard_map.275 = (bf16[608,384]{1,0:T(8,128)(2,1)}, bf16[608,384]{1,0:T(8,128)(2,1)}) custom-call(bf16[2048,576]{1,0:T(8,128)(2,1)} %get-tuple-element.116.joined, bf16[2048,768]{1,0:T(8,128)(2,1)} %get-tuple-element.117.xq), custom_call_target="tpu_custom_call" | custom-call | tf_op jit(solution)/shard_map/pallas_call | solution.py:741
  467.4 6.6 %collective-permute-done.69 = bf16[304,384]{1,0:T(8,128)(2,1)S(1)} collective-permute-done((bf16[304,384]{1,0:T(8,128)(2,1)S(1)}, bf16[304,384]{1,0:T(8,128)(2,1)S(1)}, u32[]{:S(2)}, u32[]{:S(2)}) %collective-permute-start.69) | collective-permute-done | bytes 233504 | tf_op jit(solution)/shard_map/ppermute | solution.py:536
  485.3 8.7 %shard_map.272 = (bf16[512,384]{1,0:T(8,128)(2,1)}, bf16[512,384]{1,0:T(8,128)(2,1)}) custom-call(bf16[768,384]{1,0:T(8,128)(2,1)} %get-tuple-element.105.refs_0_, bf16[768,384]{1,0:T(8,128)(2,1)} %copy-done.16, bf16[768,384]{1,0:T(8,128)(2,1)} %copy-done.17, bf16[768,384]{1,0:T(8,128)(2,1)} %collective-permute-done.63.refs_3_, bf16[1360,384]{1,0:T(8,128)(2,1)} %copy-done, ...), custom_call_target="tpu_custom_call" | custom-call | tf_op jit(solution)/shard_map/pallas_call | solution.py:743
  494.1 51.5 %psum.7 = f32[16,768]{1,0:T(8,128)S(1)} all-reduce(f32[16,768]{1,0:T(8,128)S(1)} %copy-done.49), channel_id=1, replica_groups=mesh['tok'=4,'row'=4,'col'=2] {'tok','row','col'}, use_global_device_ids=true, to_apply=%region_0.1 | all-reduce | flops 12288 | bytes 98304 | tf_op jit(solution)/shard_map/psum | solution.py:707
  567.9 8.6 %collective-permute-done.80 = bf16[768,384]{1,0:T(8,128)(2,1)S(1)} collective-permute-done((bf16[768,384]{1,0:T(8,128)(2,1)S(1)}, bf16[768,384]{1,0:T(8,128)(2,1)S(1)}, u32[]{:S(2)}, u32[]{:S(2)}) %collective-permute-start.80) | collective-permute-done | bytes 589856 | tf_op jit(solution)/shard_map/ppermute | solution.py:536
  588.7 6.8 %collective-permute-done.75 = bf16[480,384]{1,0:T(8,128)(2,1)S(1)} collective-permute-done((bf16[480,384]{1,0:T(8,128)(2,1)S(1)}, bf16[480,384]{1,0:T(8,128)(2,1)S(1)}, u32[]{:S(2)}, u32[]{:S(2)}) %collective-permute-start.75) | collective-permute-done | bytes 368672 | tf_op jit(solution)/shard_map/ppermute | solution.py:536
  597.2 5.8 collective-permute-done.82
  603.1 4.8 collective-permute-start.83
  617.1 6.0 collective-permute-done.77
  (329 shorter events, 172.1 us)
Async XLA Ops:
  43.5 21.6 %collective-permute-start.31 = (bf16[576,384]{1,0:T(8,128)(2,1)S(1)}, bf16[576,384]{1,0:T(8,128)(2,1)}, u32[]{:S(2)}, u32[]{:S(2)}) collective-permute-start(bf16[576,384]{1,0:T(8,128)(2,1)S(1)} %bitcast.28), channel_id=1, source_target_pairs={{0,1},{1,0},{2,3},{3,2},{4,5},{5,4},{6,7},{7,6},{8,9},{9,8},{10,11... | collective-permute-start | bytes 1327112 | tf_op jit(solution)/shard_map/ppermute | solution.py:536
  65.1 45.5 %collective-permute-start.49 = (bf16[1360,384]{1,0:T(8,128)(2,1)S(1)}, bf16[1360,384]{1,0:T(8,128)(2,1)S(1)}, u32[]{:S(2)}, u32[]{:S(2)}) collective-permute-start(bf16[1360,384]{1,0:T(8,128)(2,1)S(1)} %fusion.4.refs_15_.refs_4_), channel_id=1, source_target_pairs={{0,4},{2,6},{4,0},{6,2},{1,5},{3,7},{5,1},{7,3},{8,12},{10,14},{12... | collective-permute-start | bytes 3133448 | tf_op jit(solution)/shard_map/ppermute | solution.py:536
  68.8 35.0 %collective-permute-start.39 = (bf16[976,384]{1,0:T(8,128)(2,1)}, bf16[976,384]{1,0:T(8,128)(2,1)}, u32[]{:S(2)}, u32[]{:S(2)}) collective-permute-start(bf16[976,384]{1,0:T(8,128)(2,1)} %fusion.5.refs_7_), channel_id=1, source_target_pairs={{0,1},{1,0},{2,3},{3,2},{4,5},{5,4},{6,7},{7,6},{8,9},{9,8},{10,11... | collective-permute-start | bytes 2248712 | tf_op jit(solution)/shard_map/ppermute | solution.py:536
  69.2 35.1 %collective-permute-start.40 = (bf16[976,384]{1,0:T(8,128)(2,1)}, bf16[976,384]{1,0:T(8,128)(2,1)}, u32[]{:S(2)}, u32[]{:S(2)}) collective-permute-start(bf16[976,384]{1,0:T(8,128)(2,1)} %fusion.5.refs_7_), channel_id=1, source_target_pairs={{0,2},{2,0},{4,6},{6,4},{1,3},{3,1},{5,7},{7,5},{8,10},{10,8},{12,... | collective-permute-start | bytes 2248712 | tf_op jit(solution)/shard_map/ppermute | solution.py:536
  69.7 25.1 %collective-permute-start.21 = (bf16[256,384]{1,0:T(8,128)(2,1)}, bf16[256,384]{1,0:T(8,128)(2,1)S(1)}, u32[]{:S(2)}, u32[]{:S(2)}) collective-permute-start(bf16[256,384]{1,0:T(8,128)(2,1)} %copy-done.35), channel_id=1, source_target_pairs={{0,4},{2,6},{4,0},{6,2},{1,5},{3,7},{5,1},{7,3},{8,12},{10,14},{12... | collective-permute-start | bytes 589832 | tf_op jit(solution)/shard_map/ppermute | solution.py:536
  70.4 24.5 %collective-permute-start.26 = (bf16[256,384]{1,0:T(8,128)(2,1)}, bf16[256,384]{1,0:T(8,128)(2,1)S(1)}, u32[]{:S(2)}, u32[]{:S(2)}) collective-permute-start(bf16[256,384]{1,0:T(8,128)(2,1)} %copy-done.38), channel_id=1, source_target_pairs={{0,1},{1,0},{2,3},{3,2},{4,5},{5,4},{6,7},{7,6},{8,9},{9,8},{10,11... | collective-permute-start | bytes 589832 | tf_op jit(solution)/shard_map/ppermute | solution.py:536
  94.9 103.9 %collective-permute-start.42 = (bf16[976,384]{1,0:T(8,128)(2,1)}, bf16[976,384]{1,0:T(8,128)(2,1)}, u32[]{:S(2)}, u32[]{:S(2)}) collective-permute-start(bf16[976,384]{1,0:T(8,128)(2,1)} %fusion.5.refs_7_), channel_id=1, source_target_pairs={{0,4},{2,6},{4,0},{6,2},{1,5},{3,7},{5,1},{7,3},{8,12},{10,14},{12... | collective-permute-start | bytes 2248712 | tf_op jit(solution)/shard_map/ppermute | solution.py:536
  109.2 90.2 %collective-permute-start.38 = (bf16[512,384]{1,0:T(8,128)(2,1)}, bf16[512,384]{1,0:T(8,128)(2,1)S(1)}, u32[]{:S(2)}, u32[]{:S(2)}) collective-permute-start(bf16[512,384]{1,0:T(8,128)(2,1)} %get-tuple-element.87), channel_id=1, source_target_pairs={{0,1},{1,0},{2,3},{3,2},{4,5},{5,4},{6,7},{7,6},{8,9},{9,8},{10,11... | collective-permute-start | bytes 1179656 | tf_op jit(solution)/shard_map/ppermute | solution.py:536
  109.9 105.5 %collective-permute-start.47 = (bf16[1360,384]{1,0:T(8,128)(2,1)S(1)}, bf16[1360,384]{1,0:T(8,128)(2,1)S(1)}, u32[]{:S(2)}, u32[]{:S(2)}) collective-permute-start(bf16[1360,384]{1,0:T(8,128)(2,1)S(1)} %fusion.4.refs_15_.refs_4_), channel_id=1, source_target_pairs={{0,2},{2,0},{4,6},{6,4},{1,3},{3,1},{5,7},{7,5},{8,10},{10,8},{12,... | collective-permute-start | bytes 3133448 | tf_op jit(solution)/shard_map/ppermute | solution.py:536
  110.4 109.6 %collective-permute-start.46 = (bf16[1360,384]{1,0:T(8,128)(2,1)S(1)}, bf16[1360,384]{1,0:T(8,128)(2,1)}, u32[]{:S(2)}, u32[]{:S(2)}) collective-permute-start(bf16[1360,384]{1,0:T(8,128)(2,1)S(1)} %fusion.4.refs_15_.refs_4_), channel_id=1, source_target_pairs={{0,1},{1,0},{2,3},{3,2},{4,5},{5,4},{6,7},{7,6},{8,9},{9,8},{10,11... | collective-permute-start | bytes 3133448 | tf_op jit(solution)/shard_map/ppermute | solution.py:536
  110.6 109.5 %collective-permute-start.51 = (bf16[1360,384]{1,0:T(8,128)(2,1)S(1)}, bf16[1360,384]{1,0:T(8,128)(2,1)}, u32[]{:S(2)}, u32[]{:S(2)}) collective-permute-start(bf16[1360,384]{1,0:T(8,128)(2,1)S(1)} %collective-permute-done.49.refs_19_.refs_8_), channel_id=1, source_target_pairs={{0,2},{2,0},{4,6},{6,4},{1,3},{3,1},{5,7},{7,5},{8,10},{10,8},{12,... | collective-permute-start | bytes 3133448 | tf_op jit(solution)/shard_map/ppermute | solution.py:536
  285.7 168.7 %collective-permute-start.72 = (bf16[4,960,384]{2,1,0:T(8,128)(2,1)}, bf16[4,960,384]{2,1,0:T(8,128)(2,1)}, u32[]{:S(2)}, u32[]{:S(2)}) collective-permute-start(bf16[4,960,384]{2,1,0:T(8,128)(2,1)} %get-tuple-element.126), channel_id=1, source_target_pairs={{0,1},{1,0},{2,3},{3,2},{4,5},{5,4},{6,7},{7,6},{8,9},{9,8},{10,11... | collective-permute-start | bytes 8847368 | tf_op jit(solution)/shard_map/ppermute | solution.py:536
  404.6 24.9 %collective-permute-start.60 = (bf16[3,2048,128]{2,1,0:T(8,128)(2,1)}, bf16[3,2048,128]{2,1,0:T(8,128)(2,1)S(1)}, u32[]{:S(2)}, u32[]{:S(2)}) collective-permute-start(bf16[3,2048,128]{2,1,0:T(8,128)(2,1)} %get-tuple-element.104), channel_id=1, source_target_pairs={{0,1},{1,0},{2,3},{3,2},{4,5},{5,4},{6,7},{7,6},{8,9},{9,8},{10,11... | collective-permute-start | bytes 4718600 | tf_op jit(solution)/shard_map/ppermute | solution.py:536
  424.7 34.1 %collective-permute-start.78 = (bf16[4,768,384]{2,1,0:T(8,128)(2,1)}, bf16[4,768,384]{2,1,0:T(8,128)(2,1)}, u32[]{:S(2)}, u32[]{:S(2)}) collective-permute-start(bf16[4,768,384]{2,1,0:T(8,128)(2,1)} %get-tuple-element.129), channel_id=1, source_target_pairs={{0,1},{1,0},{2,3},{3,2},{4,5},{5,4},{6,7},{7,6},{8,9},{9,8},{10,11... | collective-permute-start | bytes 7077896 | tf_op jit(solution)/shard_map/ppermute | solution.py:536
  451.8 28.8 %collective-permute-start.62 = (bf16[768,384]{1,0:T(8,128)(2,1)}, bf16[768,384]{1,0:T(8,128)(2,1)S(1)}, u32[]{:S(2)}, u32[]{:S(2)}) collective-permute-start(bf16[768,384]{1,0:T(8,128)(2,1)} %get-tuple-element.107), channel_id=1, source_target_pairs={{0,4},{2,6},{4,0},{6,2},{1,5},{3,7},{5,1},{7,3},{8,12},{10,14},{12... | collective-permute-start | bytes 1769480 | tf_op jit(solution)/shard_map/ppermute | solution.py:536
  454.4 30.9 %collective-permute-start.63 = (bf16[768,384]{1,0:T(8,128)(2,1)}, bf16[768,384]{1,0:T(8,128)(2,1)}, u32[]{:S(2)}, u32[]{:S(2)}) collective-permute-start(bf16[768,384]{1,0:T(8,128)(2,1)} %get-tuple-element.108), channel_id=1, source_target_pairs={{0,6},{2,4},{4,2},{6,0},{1,7},{3,5},{5,3},{7,1},{8,14},{10,12},{12... | collective-permute-start | bytes 1769480 | tf_op jit(solution)/shard_map/ppermute | solution.py:536
  458.8 104.4 %collective-permute-start.73 = (bf16[2,960,384]{2,1,0:T(8,128)(2,1)}, bf16[2,960,384]{2,1,0:T(8,128)(2,1)}, u32[]{:S(2)}, u32[]{:S(2)}) collective-permute-start(bf16[2,960,384]{2,1,0:T(8,128)(2,1)} %add_convert_fusion), channel_id=1, source_target_pairs={{0,2},{2,0},{4,6},{6,4},{1,3},{3,1},{5,7},{7,5},{8,10},{10,8},{12,... | collective-permute-start | bytes 4423688 | tf_op jit(solution)/shard_map/ppermute | solution.py:536
  462.1 96.4 %collective-permute-start.79 = (bf16[2,768,384]{2,1,0:T(8,128)(2,1)}, bf16[2,768,384]{2,1,0:T(8,128)(2,1)}, u32[]{:S(2)}, u32[]{:S(2)}) collective-permute-start(bf16[2,768,384]{2,1,0:T(8,128)(2,1)} %add_convert_fusion.1), channel_id=1, source_target_pairs={{0,4},{2,6},{4,0},{6,2},{1,5},{3,7},{5,1},{7,3},{8,12},{10,14},{12... | collective-permute-start | bytes 3538952 | tf_op jit(solution)/shard_map/ppermute | solution.py:536
  481.4 70.1 %collective-permute-start.70 = (bf16[304,384]{1,0:T(8,128)(2,1)S(1)}, bf16[304,384]{1,0:T(8,128)(2,1)S(1)}, u32[]{:S(2)}, u32[]{:S(2)}) collective-permute-start(bf16[304,384]{1,0:T(8,128)(2,1)S(1)} %add_convert_fusion.10), channel_id=1, source_target_pairs={{0,24},{8,16},{16,8},{24,0},{1,25},{9,17},{17,9},{25,1},{2,26},{10... | collective-permute-start | bytes 700424 | tf_op jit(solution)/shard_map/ppermute | solution.py:536
  485.3 61.7 %collective-permute-start.56 = (bf16[256,384]{1,0:T(8,128)(2,1)}, bf16[256,384]{1,0:T(8,128)(2,1)}, u32[]{:S(2)}, u32[]{:S(2)}) collective-permute-start(bf16[256,384]{1,0:T(8,128)(2,1)} %get-tuple-element.93), channel_id=1, source_target_pairs={{0,24},{8,0},{16,8},{24,16},{1,25},{9,1},{17,9},{25,17},{2,26},{10... | collective-permute-start | bytes 589832 | tf_op jit(solution)/shard_map/ppermute | solution.py:536
  494.0 57.6 %collective-permute-start.64 = (bf16[512,384]{1,0:T(8,128)(2,1)}, bf16[512,384]{1,0:T(8,128)(2,1)}, u32[]{:S(2)}, u32[]{:S(2)}) collective-permute-start(bf16[512,384]{1,0:T(8,128)(2,1)} %get-tuple-element.111), channel_id=1, source_target_pairs={{0,1},{1,0},{2,3},{3,2},{4,5},{5,4},{6,7},{7,6},{8,9},{9,8},{10,11... | collective-permute-start | bytes 1179656 | tf_op jit(solution)/shard_map/ppermute | solution.py:536
  556.4 53.1 %collective-permute-start.65 = (bf16[256,384]{1,0:T(8,128)(2,1)}, bf16[256,384]{1,0:T(8,128)(2,1)}, u32[]{:S(2)}, u32[]{:S(2)}) collective-permute-start(bf16[256,384]{1,0:T(8,128)(2,1)} %get-tuple-element.113), channel_id=1, source_target_pairs={{0,8},{8,16},{16,24},{24,0},{1,9},{9,17},{17,25},{25,1},{2,10},{10... | collective-permute-start | bytes 589832 | tf_op jit(solution)/shard_map/ppermute | solution.py:536
  558.4 51.1 %collective-permute-start.66 = (bf16[256,384]{1,0:T(8,128)(2,1)}, bf16[256,384]{1,0:T(8,128)(2,1)}, u32[]{:S(2)}, u32[]{:S(2)}) collective-permute-start(bf16[256,384]{1,0:T(8,128)(2,1)} %get-tuple-element.114), channel_id=1, source_target_pairs={{0,16},{8,24},{16,0},{24,8},{1,17},{9,25},{17,1},{25,9},{2,18},{10... | collective-permute-start | bytes 589832 | tf_op jit(solution)/shard_map/ppermute | solution.py:536
  558.5 50.9 %collective-permute-start.67 = (bf16[256,384]{1,0:T(8,128)(2,1)}, bf16[256,384]{1,0:T(8,128)(2,1)}, u32[]{:S(2)}, u32[]{:S(2)}) collective-permute-start(bf16[256,384]{1,0:T(8,128)(2,1)} %get-tuple-element.115), channel_id=1, source_target_pairs={{0,24},{8,0},{16,8},{24,16},{1,25},{9,1},{17,9},{25,17},{2,26},{10... | collective-permute-start | bytes 589832 | tf_op jit(solution)/shard_map/ppermute | solution.py:536
  (121 other events, 1787.9 us)
